TPU v7x, 256 devices: a whole 4x4x8 slice. The times are simulated.
256 devices in a mesh: pipe: 16 (over y, z_hi), ep: 16 (over z_lo, x, core).
Axes of the slice: x: 4, y: 4, z: 8 (z_hi: 4, z_lo: 2; z = z_hi * 2 + z_lo), core: 2. Of those that a mesh axis runs over, the one named last changes fastest.
Arguments:
- forward_states: bfloat16 [16, 1024, 7168], P('pipe', 'ep'), may hold values from -6 to 6
- reverse_states: bfloat16 [16, 1024, 7168], P('pipe', 'ep'), may hold values from -6 to 6
- forward_routes: int32 [1, 16, 1024, 1], P(None, 'pipe'), may hold values from 0 to 1; in each aligned block of 64 rows (0 to 63, 64 to 127, ..., all dimensions but the last counted through in order) at most 32 rows name the same one
- reverse_routes: int32 [1, 16, 1024, 1], P(None, 'pipe'), may hold values from 0 to 1; in each aligned block of 64 rows (0 to 63, 64 to 127, ..., all dimensions but the last counted through in order) at most 32 rows name the same one
- forward_share: float32 [1, 16, 1024], P(None, 'pipe', 'ep'), may hold values from 0.2 to 2.5
- reverse_share: float32 [1, 16, 1024], P(None, 'pipe', 'ep'), may hold values from 0.2 to 2.5
- layer_gate: bfloat16 [16, 7168, 2048], P('pipe', None, 'ep'), may hold values from -0.0625 to 0.0625
- layer_up: bfloat16 [16, 7168, 2048], P('pipe', None, 'ep'), may hold values from -0.0625 to 0.0625
- layer_down: bfloat16 [16, 2048, 7168], P('pipe', 'ep'), may hold values from -0.1875 to 0.1875
Outputs:
- forward_out: bfloat16 [16, 1024, 7168], P('pipe', 'ep')
- reverse_out: bfloat16 [16, 1024, 7168], P('pipe', 'ep')
Inputs may be any that keep to these rules, and one draw needn't show every extreme that they name: `forward_routes`: in each step, section and aligned block of 64 tokens (the tokens of one device), exactly 32 tokens name each expert. `reverse_routes`: in each step, section and aligned block of 64 tokens (the tokens of one device), exactly 32 tokens name each expert.
All inputs are finite; a program needn't handle non-finite values.
Results may differ from a plain program's by a relative error of at most 0.0052.
Values may be sent and summed in bfloat16 or wider, within the bound.
No kernel may reach another device: no remote copies, remote signals or barrier semaphores. Data moves between devices by JAX's collectives and lax.ppermute only.
A program may use at most 128 MiB of HBM per device.

v0:
```python
import jax
import jax.numpy as jnp
from jax import lax
from jax.sharding import PartitionSpec as P

EXPERTS = 2


def shifted(shard, axis, by):
    peers = lax.axis_size(axis)
    pairs = [(i, i + by) for i in range(peers) if 0 <= i + by < peers]
    return lax.ppermute(shard, axis, pairs)


def slot_table(routes_local, capacity):
    count = routes_local.shape[0]
    onehot = (routes_local[:, None] == jnp.arange(EXPERTS, dtype=jnp.int32)[None, :]).astype(
        jnp.int32
    )
    rank = jnp.sum(jnp.cumsum(onehot, axis=0) * onehot, axis=1) - 1
    slot = routes_local * capacity + rank
    holder = (
        jnp.zeros((EXPERTS * capacity,), jnp.int32).at[slot].set(jnp.arange(count, dtype=jnp.int32))
    )
    return (slot, holder)


def pack_rows(states, holder, capacity, slices):
    packed = states[holder]
    packed = packed.reshape(EXPERTS, capacity, states.shape[1])
    return jnp.repeat(packed, slices, axis=0)


def expert_rows(rows, gate, up, down):
    flat = rows.reshape(-1, rows.shape[2])
    gated = jnp.dot(flat, gate, preferred_element_type=jnp.float32)
    upward = jnp.dot(flat, up, preferred_element_type=jnp.float32)
    hidden = (jax.nn.silu(gated) * upward).astype(jnp.bfloat16)
    partial_rows = jnp.dot(hidden, down, preferred_element_type=jnp.float32).astype(jnp.bfloat16)
    return partial_rows.reshape(rows.shape)


def finish(states, returned, slot, share, capacity, slices):
    width = states.shape[1]
    summed = jnp.sum(returned.reshape(EXPERTS, slices, capacity, width), axis=1, dtype=jnp.float32)
    summed = summed.reshape(EXPERTS * capacity, width)
    branch = summed[slot]
    return (states.astype(jnp.float32) + share[:, None] * branch).astype(jnp.bfloat16)


def one_way(outgoing, gate, up, down):
    return lax.all_to_all(
        expert_rows(
            lax.all_to_all(outgoing, "ep", split_axis=0, concat_axis=0, tiled=True), gate, up, down
        ),
        "ep",
        split_axis=0,
        concat_axis=0,
        tiled=True,
    )


def per_device(
    forward_states,
    reverse_states,
    forward_routes,
    reverse_routes,
    forward_share,
    reverse_share,
    layer_gate,
    layer_up,
    layer_down,
):
    ranks = lax.axis_size("ep")
    mine = lax.axis_index("ep")
    slices = ranks // EXPERTS
    count = forward_states.shape[1]
    capacity = count // EXPERTS
    gate = layer_gate[0]
    up = layer_up[0]
    down = layer_down[0]
    ahead = forward_states[0]
    behind = reverse_states[0]
    routes_ahead = lax.dynamic_slice_in_dim(forward_routes[0, 0, :, 0], mine * count, count)
    routes_behind = lax.dynamic_slice_in_dim(reverse_routes[0, 0, :, 0], mine * count, count)
    slot_ahead, holder_ahead = slot_table(routes_ahead, capacity)
    slot_behind, holder_behind = slot_table(routes_behind, capacity)
    outgoing_ahead = pack_rows(ahead, holder_ahead, capacity, slices)
    outgoing_behind = pack_rows(behind, holder_behind, capacity, slices)
    back_ahead = one_way(outgoing_ahead, gate, up, down)
    back_behind = one_way(outgoing_behind, gate, up, down)
    result_ahead = finish(ahead, back_ahead, slot_ahead, forward_share[0, 0], capacity, slices)
    result_behind = finish(behind, back_behind, slot_behind, reverse_share[0, 0], capacity, slices)
    ahead = shifted(result_ahead, "pipe", 1)
    behind = shifted(result_behind, "pipe", -1)
    return (ahead[None], behind[None])


def solution(mesh):
    in_specs = (
        P("pipe", "ep", None),
        P("pipe", "ep", None),
        P(None, "pipe", None, None),
        P(None, "pipe", None, None),
        P(None, "pipe", "ep"),
        P(None, "pipe", "ep"),
        P("pipe", None, "ep"),
        P("pipe", None, "ep"),
        P("pipe", "ep", None),
    )
    out_specs = (P("pipe", "ep", None), P("pipe", "ep", None))
    return jax.shard_map(
        per_device, mesh=mesh, in_specs=in_specs, out_specs=out_specs, check_vma=False
    )
```

profile of v0, /device:TPU:31, one launch (start us, length us, event | category | flops | bytes accessed | tf_op | source)
XLA Modules:
  0.0 548.9 jit_solution(2058693108313372971)
XLA Ops:
  6.0 3.3 gather_fusion.2
  9.3 3.9 broadcast_in_dim.30
  13.2 6.6 %all-to-all-start.2 = ((bf16[16,32,7168]{2,1,0:T(8,128)(2,1)}), bf16[16,32,7168]{2,1,0:T(8,128)(2,1)}, u32[]{:S(2)}, u32[]{:S(2)}) async-start(bf16[16,32,7168]{2,1,0:T(8,128)(2,1)} %bitcast.81), calls=%async_computation.2 | async-start | bytes 14680064 | tf_op jit(solution)/shard_map/all_to_all | solution.py:54
  21.9 109.5 %all-to-all-done.2 = bf16[16,32,7168]{2,1,0:T(8,128)(2,1)} async-done(((bf16[16,32,7168]{2,1,0:T(8,128)(2,1)}), bf16[16,32,7168]{2,1,0:T(8,128)(2,1)}, u32[]{:S(2)}, u32[]{:S(2)}) %all-to-all-start.2) | async-done | bytes 7340064 | tf_op jit(solution)/shard_map/all_to_all | solution.py:54
  131.3 5.1 broadcast_in_dim.13
  136.4 5.4 all-to-all-start
  141.8 5.6 %fusion.6 = f32[512,128]{1,0:T(8,128)S(1)} fusion(bf16[512,7168]{1,0:T(8,128)(2,1)} %bitcast.24, bf16[1,7168,128]{2,1,0:T(8,128)(2,1)} %param.15), kind=kOutput, calls=%fused_computation.16 | convolution fusion | flops 939524096 | bytes 9437184 | tf_op jit(solution)/shard_map/dot_general | solution.py:36
  147.4 15.2 %convolution_convert_fusion = bf16[512,7168]{1,0:T(8,128)(2,1)} fusion(bf16[1,128,7168]{2,1,0:T(8,128)(2,1)S(1)} %copy-done, bf16[512,7168]{1,0:T(8,128)(2,1)} %bitcast.24, bf16[1,7168,128]{2,1,0:T(8,128)(2,1)} %param.16, f32[512,128]{1,0:T(8,128)S(1)} %fusion.6), kind=kOutput, calls=%fused_computation.8 | convolution fusion | flops 1883111424 | bytes 18612224 | tf_op jit(solution)/shard_map/dot_general | solution.py:39
  162.6 90.7 %all-to-all-done = bf16[16,32,7168]{2,1,0:T(8,128)(2,1)} async-done(((bf16[16,32,7168]{2,1,0:T(8,128)(2,1)}), bf16[16,32,7168]{2,1,0:T(8,128)(2,1)}, u32[]{:S(2)}, u32[]{:S(2)}) %all-to-all-start) | async-done | bytes 7340064 | tf_op jit(solution)/shard_map/all_to_all | solution.py:54
  253.3 5.4 all-to-all-start.3
  258.7 5.6 %fusion.8 = f32[512,128]{1,0:T(8,128)S(1)} fusion(bf16[512,7168]{1,0:T(8,128)(2,1)} %bitcast.8, bf16[1,7168,128]{2,1,0:T(8,128)(2,1)} %param.15), kind=kOutput, calls=%fused_computation.18 | convolution fusion | flops 939524096 | bytes 9437184 | tf_op jit(solution)/shard_map/dot_general | solution.py:36
  264.3 15.2 %convolution_convert_fusion.1 = bf16[512,7168]{1,0:T(8,128)(2,1)} fusion(bf16[1,128,7168]{2,1,0:T(8,128)(2,1)S(1)} %copy-done, bf16[512,7168]{1,0:T(8,128)(2,1)} %bitcast.8, bf16[1,7168,128]{2,1,0:T(8,128)(2,1)} %param.16, f32[512,128]{1,0:T(8,128)S(1)} %fusion.8), kind=kOutput, calls=%fused_computation.9 | convolution fusion | flops 1883111424 | bytes 18612224 | tf_op jit(solution)/shard_map/dot_general | solution.py:39
  279.6 90.7 %all-to-all-done.3 = bf16[16,32,7168]{2,1,0:T(8,128)(2,1)} async-done(((bf16[16,32,7168]{2,1,0:T(8,128)(2,1)}), bf16[16,32,7168]{2,1,0:T(8,128)(2,1)}, u32[]{:S(2)}, u32[]{:S(2)}) %all-to-all-start.3) | async-done | bytes 7340064 | tf_op jit(solution)/shard_map/all_to_all | solution.py:52
  370.2 5.4 all-to-all-start.1
  375.6 4.5 convert_reduce_fusion
  380.1 2.3 gather_fusion.3
  382.4 2.7 add_convert_fusion
  385.1 7.2 %collective-permute-start.1 = (bf16[64,7168]{1,0:T(8,128)(2,1)}, bf16[64,7168]{1,0:T(8,128)(2,1)}, u32[]{:S(2)}, u32[]{:S(2)}) collective-permute-start(bf16[64,7168]{1,0:T(8,128)(2,1)} %add_convert_fusion), channel_id=1, source_target_pairs={{16,0},{32,16},{48,32},{64,48},{80,64},{96,80},{112,96},{128,112},... | collective-permute-start | bytes 2752520 | tf_op jit(solution)/shard_map/ppermute | solution.py:12
  392.3 107.8 %all-to-all-done.1 = bf16[16,32,7168]{2,1,0:T(8,128)(2,1)} async-done(((bf16[16,32,7168]{2,1,0:T(8,128)(2,1)}), bf16[16,32,7168]{2,1,0:T(8,128)(2,1)}, u32[]{:S(2)}, u32[]{:S(2)}) %all-to-all-start.1) | async-done | bytes 7340064 | tf_op jit(solution)/shard_map/all_to_all | solution.py:52
  500.1 4.4 convert_reduce_fusion.1
  504.6 2.3 gather_fusion.1
  508.7 4.9 collective-permute-start
  513.6 32.2 %collective-permute-done = bf16[64,7168]{1,0:T(8,128)(2,1)S(1)} collective-permute-done((bf16[64,7168]{1,0:T(8,128)(2,1)S(1)}, bf16[64,7168]{1,0:T(8,128)(2,1)S(1)}, u32[]{:S(2)}, u32[]{:S(2)}) %collective-permute-start) | collective-permute-done | bytes 917536 | tf_op jit(solution)/shard_map/ppermute | solution.py:12
  546.8 2.2 copy.14
  (37 shorter events, 10.1 us)
Async XLA Ops:
  0.6 146.8 %copy-start = (bf16[1,128,7168]{2,1,0:T(8,128)(2,1)S(1)}, bf16[1,128,7168]{2,1,0:T(8,128)(2,1)}, u32[]{:S(2)}) copy-start(bf16[1,128,7168]{2,1,0:T(8,128)(2,1)} %param.17) | copy-start | bytes 5505028
  13.2 6.6 %copy-start.3 = (bf16[1,64,7168]{2,1,0:T(8,128)(2,1)S(1)}, bf16[1,64,7168]{2,1,0:T(8,128)(2,1)}, u32[]{:S(2)}) copy-start(bf16[1,64,7168]{2,1,0:T(8,128)(2,1)} %param.9) | copy-start | bytes 2752516
  13.2 118.1 %all-to-all-start.2 = ((bf16[16,32,7168]{2,1,0:T(8,128)(2,1)}), bf16[16,32,7168]{2,1,0:T(8,128)(2,1)}, u32[]{:S(2)}, u32[]{:S(2)}) async-start(bf16[16,32,7168]{2,1,0:T(8,128)(2,1)} %bitcast.81), calls=%async_computation.2 | async-start | bytes 14680064 | tf_op jit(solution)/shard_map/all_to_all | solution.py:54
  136.4 116.9 %all-to-all-start = ((bf16[16,32,7168]{2,1,0:T(8,128)(2,1)}), bf16[16,32,7168]{2,1,0:T(8,128)(2,1)}, u32[]{:S(2)}, u32[]{:S(2)}) async-start(bf16[16,32,7168]{2,1,0:T(8,128)(2,1)} %bitcast.82), calls=%async_computation | async-start | bytes 14680064 | tf_op jit(solution)/shard_map/all_to_all | solution.py:54
  253.3 116.9 %all-to-all-start.3 = ((bf16[16,32,7168]{2,1,0:T(8,128)(2,1)}), bf16[16,32,7168]{2,1,0:T(8,128)(2,1)}, u32[]{:S(2)}, u32[]{:S(2)}) async-start(bf16[16,32,7168]{2,1,0:T(8,128)(2,1)} %bitcast.80), calls=%async_computation.3 | async-start | bytes 14680064 | tf_op jit(solution)/shard_map/all_to_all | solution.py:52
  370.2 129.9 %all-to-all-start.1 = ((bf16[16,32,7168]{2,1,0:T(8,128)(2,1)}), bf16[16,32,7168]{2,1,0:T(8,128)(2,1)}, u32[]{:S(2)}, u32[]{:S(2)}) async-start(bf16[16,32,7168]{2,1,0:T(8,128)(2,1)} %bitcast.79), calls=%async_computation.1 | async-start | bytes 14680064 | tf_op jit(solution)/shard_map/all_to_all | solution.py:52
  380.1 2.4 copy-start.2
  380.1 2.4 copy-start.5
  385.1 128.5 %collective-permute-start.1 = (bf16[64,7168]{1,0:T(8,128)(2,1)}, bf16[64,7168]{1,0:T(8,128)(2,1)}, u32[]{:S(2)}, u32[]{:S(2)}) collective-permute-start(bf16[64,7168]{1,0:T(8,128)(2,1)} %add_convert_fusion), channel_id=1, source_target_pairs={{16,0},{32,16},{48,32},{64,48},{80,64},{96,80},{112,96},{128,112},... | collective-permute-start | bytes 2752520 | tf_op jit(solution)/shard_map/ppermute | solution.py:12
  504.6 2.4 copy-start.4
  504.6 2.4 copy-start.6
  508.7 37.1 %collective-permute-start = (bf16[64,7168]{1,0:T(8,128)(2,1)S(1)}, bf16[64,7168]{1,0:T(8,128)(2,1)S(1)}, u32[]{:S(2)}, u32[]{:S(2)}) collective-permute-start(bf16[64,7168]{1,0:T(8,128)(2,1)S(1)} %add_convert_fusion.1), channel_id=1, source_target_pairs={{0,16},{16,32},{32,48},{48,64},{64,80},{80,96},{96,112},{112,128},... | collective-permute-start | bytes 2752520 | tf_op jit(solution)/shard_map/ppermute | solution.py:12
  545.8 3.1 copy-start.1
where the time goes:
time: 550 us; the launch traced here: 549 us
  waiting for transfers between devices  431 us (78%)
  matrix products  41.7 us (8%)
  starting transfers between devices  34.8 us (6%)
  local copies, waits for them, and re-layouts  25.3 us (5%)
  other arithmetic  15.6 us (3%)
    all_to_all x2, waiting for transfers between devices, one_way(): lax.all_to_all(outgoing, 'ep', split_axis=0, concat_axis=0, tiled=True)  200 us
    all_to_all x2, waiting for transfers between devices, one_way(): lax.all_to_all(expert_rows(lax.all_to_all(outgoing, 'ep', split_axis=0, c...  198 us
    ppermute x2, waiting for transfers between devices, shifted(): return lax.ppermute(shard, axis, pairs)  32.2 us
    dot_general x2, matrix products, expert_rows(): jnp.dot(hidden, down, preferred_element_type=jnp.float32)  30.4 us
    ppermute x2, starting transfers between devices, shifted(): return lax.ppermute(shard, axis, pairs)  12.1 us
    all_to_all x2, starting transfers between devices, one_way(): lax.all_to_all(outgoing, 'ep', split_axis=0, concat_axis=0, tiled=True)  12 us
    dot_general x2, matrix products, expert_rows(): gated = jnp.dot(flat, gate, preferred_element_type=jnp.float32)  11.3 us
  transfers between devices with their start and end apart: 6, of which 5 were waited for; matrix products, arithmetic and copies ran while one was open for 11% of the time, Pallas kernels for 0%

commit v1 on v0

v1 whole, which is shorter than its diff:
```python
import functools

import jax
import jax.numpy as jnp
from jax import lax
from jax.experimental import pallas as pl
from jax.experimental.pallas import tpu as pltpu
from jax.sharding import PartitionSpec as P

EXPERTS = 2
RING = 4
CORES = 2
OFFSETS = (0, -1, 1, 2)
PLACE = {offset % RING: at for at, offset in enumerate(OFFSETS)}
VMEM_LIMIT = 16 * 1024 * 1024


def move(shard, pipes, by=0, flip=False, steps=0, core=False):
    pairs = []
    for pipe in range(pipes):
        if not 0 <= pipe + by < pipes:
            continue
        for z in range(EXPERTS):
            for x in range(RING):
                for c in range(CORES):
                    source = ((pipe * EXPERTS + z) * RING + x) * CORES + c
                    z_to = 1 - z if flip else z
                    x_to = (x + steps) % RING
                    c_to = 1 - c if core else c
                    pairs.append(
                        (source, (((pipe + by) * EXPERTS + z_to) * RING + x_to) * CORES + c_to)
                    )
    return lax.ppermute(shard, ("pipe", "ep"), pairs)


def picks(routes, expert, capacity):
    count = routes.shape[1]
    match = (routes == expert).astype(jnp.float32)
    upto = (
        lax.broadcasted_iota(jnp.int32, (count, count), 0)
        <= lax.broadcasted_iota(jnp.int32, (count, count), 1)
    ).astype(jnp.float32)
    rank = jnp.dot(match, upto, preferred_element_type=jnp.float32)
    slots = lax.broadcasted_iota(jnp.int32, (capacity, count), 0).astype(jnp.float32) + 1.0
    return jnp.where((rank == slots) & (match > 0.0), 1.0, 0.0)


def slices_kernel(x_ref, down, *refs):
    outs, sems = refs[:-1], refs[-1]
    columns = outs[0].shape[1]
    copies = []
    for at, (offset, out) in enumerate(zip(OFFSETS, outs)):
        start = pl.multiple_of(lax.rem(x_ref[0] - offset + RING, RING) * columns, 128)
        copies.append(
            pltpu.make_async_copy(down.at[:, pl.ds(start, columns)], out, sems.at[at])
        )
    for copy in copies:
        copy.start()
    for copy in copies:
        copy.wait()


def slices(x, down):
    depth, width = down.shape
    return pl.pallas_call(
        slices_kernel,
        in_specs=[
            pl.BlockSpec(memory_space=pltpu.SMEM),
            pl.BlockSpec(memory_space=pltpu.HBM),
        ],
        out_specs=[pl.BlockSpec(memory_space=pltpu.VMEM)] * RING,
        out_shape=[jax.ShapeDtypeStruct((depth, width // RING), down.dtype)] * RING,
        scratch_shapes=[pltpu.SemaphoreType.DMA((RING,))],
        compiler_params=pltpu.CompilerParams(vmem_limit_bytes=VMEM_LIMIT),
        name="slices",
    )(x, pltpu.with_memory_space_constraint(down, pltpu.HBM))


def pack_kernel(place, fr, rr, fs, rs, fx, rx, *refs):
    (own_f, own_r, oth, fr_v, rr_v, fs_v, rs_v, fx_v, rx_v, sems) = refs
    count, width = fx.shape
    capacity = count // EXPERTS
    copies = [
        pltpu.make_async_copy(source, target, sems.at[at])
        for at, (source, target) in enumerate(
            ((fr, fr_v), (rr, rr_v), (fs, fs_v), (rs, rs_v), (fx, fx_v), (rx, rx_v))
        )
    ]
    for copy in copies:
        copy.start()
    mine, z = place[0], place[1]
    every = fr.shape[1]
    lane = lax.broadcasted_iota(jnp.int32, (capacity, 128), 1)
    token = lax.broadcasted_iota(jnp.int32, (capacity, count), 1).astype(jnp.float32)
    local = (
        lax.broadcasted_iota(jnp.int32, (every, count), 0)
        == lax.broadcasted_iota(jnp.int32, (every, count), 1) + mine * count
    ).astype(jnp.bfloat16)
    for copy in copies[:4]:
        copy.wait()
    found = []
    for routes, share in ((fr_v, fs_v), (rr_v, rs_v)):
        routes = jnp.dot(
            routes[...].astype(jnp.bfloat16), local, preferred_element_type=jnp.float32
        )
        routes = (routes > 0.5).astype(jnp.int32)
        for expert in (z, 1 - z):
            pick = picks(routes, expert, capacity)
            rest = jnp.sum(pick * share[...], axis=1, keepdims=True)
            tail = jnp.where(lane == 3, jnp.sum(pick * token, axis=1, keepdims=True), 0.0)
            for at_term in range(3):
                term = rest.astype(jnp.bfloat16).astype(jnp.float32)
                tail = jnp.where(lane == at_term, term, tail)
                rest = rest - term
            found.append((pick.astype(jnp.bfloat16), tail.astype(jnp.bfloat16)))
    for at, rows in enumerate((fx_v, rx_v)):
        copies[4 + at].wait()
        for side in range(2):
            pick, tail = found[2 * at + side]
            out = oth if side else (own_f, own_r)[at]
            part = slice(at * capacity, (at + 1) * capacity) if side else slice(None)
            out[part, :width] = jnp.dot(
                pick, rows[...], preferred_element_type=jnp.float32
            ).astype(jnp.bfloat16)
            out[part, width:] = tail


def pack(place, *arrays):
    count, width = arrays[4].shape
    every = arrays[0].shape[1]
    return pl.pallas_call(
        pack_kernel,
        in_specs=[pl.BlockSpec(memory_space=pltpu.SMEM)]
        + [pl.BlockSpec(memory_space=pltpu.HBM)] * 6,
        out_specs=[pl.BlockSpec(memory_space=pltpu.VMEM)] * 3,
        out_shape=[
            jax.ShapeDtypeStruct((rows, width + 128), jnp.bfloat16)
            for rows in (count // 2, count // 2, count)
        ],
        scratch_shapes=[pltpu.VMEM((1, every), jnp.int32)] * 2
        + [pltpu.VMEM((1, count), jnp.float32)] * 2
        + [pltpu.VMEM((count, width), jnp.bfloat16)] * 2
        + [pltpu.SemaphoreType.DMA((6,))],
        compiler_params=pltpu.CompilerParams(vmem_limit_bytes=VMEM_LIMIT),
        name="pack",
    )(place, *[pltpu.with_memory_space_constraint(a, pltpu.HBM) for a in arrays])


def hidden_kernel(steps, *refs):
    rows, (go, gt, uo, ut), (out, gated, upward) = refs[:-7], refs[-7:-3], refs[-3:]
    block = go.shape[0] // steps

    def step(at, _):
        part = pl.ds(pl.multiple_of(at * block, 128), block)
        x = jnp.concatenate([r[:, part] for r in rows], axis=0)
        g = jnp.concatenate([go[part, :], gt[part, :]], axis=1)
        u = jnp.concatenate([uo[part, :], ut[part, :]], axis=1)
        gated[...] += jnp.dot(x, g, preferred_element_type=jnp.float32)
        upward[...] += jnp.dot(x, u, preferred_element_type=jnp.float32)
        return 0

    gated[...] = jnp.zeros_like(gated)
    upward[...] = jnp.zeros_like(upward)
    lax.fori_loop(0, steps, step, 0, unroll=True)
    out[...] = (jax.nn.silu(gated[...]) * upward[...]).astype(jnp.bfloat16)


def hidden_rows(rows, weights):
    width, lanes = weights[0].shape
    count = sum(r.shape[0] for r in rows)
    whole = pl.BlockSpec(memory_space=pltpu.VMEM)
    return pl.pallas_call(
        functools.partial(hidden_kernel, 7),
        in_specs=[whole] * (len(rows) + 4),
        out_specs=whole,
        out_shape=jax.ShapeDtypeStruct((count, 2 * lanes), jnp.bfloat16),
        scratch_shapes=[pltpu.VMEM((count, 2 * lanes), jnp.float32)] * 2,
        compiler_params=pltpu.CompilerParams(vmem_limit_bytes=VMEM_LIMIT),
        cost_estimate=pl.CostEstimate(
            flops=8 * count * width * lanes,
            bytes_accessed=2 * width * (count + 4 * lanes),
            transcendentals=count * 2 * lanes,
        ),
        name="hidden",
    )(*rows, *weights)


def out_kernel(steps, x_ref, *refs):
    rows, hidden, down, outs, h = refs[:8], refs[8:12], refs[12:14], refs[14:18], refs[18]
    pair = 2 * rows[0].shape[0]
    lanes = hidden[0].shape[1] // 2
    columns = down[0].shape[1]
    width = RING * columns
    block = columns // steps
    for at, o in enumerate(OFFSETS):
        for core in range(CORES):
            for index, (s, source) in enumerate(zip(OFFSETS, hidden)):
                place = PLACE[(o - s) % RING]
                h[
                    at * pair : (at + 1) * pair,
                    (core * RING + index) * lanes : (core * RING + index + 1) * lanes,
                ] = source[place * pair : (place + 1) * pair, core * lanes : (core + 1) * lanes]
    terms = jnp.concatenate([r[:, width:] for r in rows], axis=0).astype(jnp.float32)
    share = terms[:, 0:1] + terms[:, 1:2] + terms[:, 2:3]

    def step(j, _):
        part = pl.ds(pl.multiple_of(j * block, 128), block)
        there = pl.ds(pl.multiple_of(x_ref[0] * columns + j * block, 128), block)
        d = jnp.concatenate([r[:, part] for r in down], axis=0)
        branch = jnp.dot(h[...], d, preferred_element_type=jnp.float32)
        states = jnp.concatenate([r[:, there] for r in rows], axis=0).astype(jnp.float32)
        result = (states + share * branch).astype(jnp.bfloat16)
        for at, out in enumerate(outs):
            out[:, part] = result[at * pair : (at + 1) * pair]
        return 0

    lax.fori_loop(0, steps, step, 0, unroll=True)


def out_rows(x, rows, hidden, down):
    half, wide = rows[0].shape
    pair = 2 * half
    count = RING * pair
    columns = (wide - 128) // RING
    lanes = hidden[0].shape[1]
    whole = pl.BlockSpec(memory_space=pltpu.VMEM)
    return pl.pallas_call(
        functools.partial(out_kernel, 7),
        in_specs=[pl.BlockSpec(memory_space=pltpu.SMEM)] + [whole] * 14,
        out_specs=[whole] * 4,
        out_shape=[jax.ShapeDtypeStruct((pair, columns), jnp.bfloat16)] * 4,
        scratch_shapes=[pltpu.VMEM((count, RING * lanes), jnp.bfloat16)],
        compiler_params=pltpu.CompilerParams(vmem_limit_bytes=VMEM_LIMIT),
        cost_estimate=pl.CostEstimate(
            flops=2 * count * columns * 4 * lanes,
            bytes_accessed=2 * columns * (2 * count + 4 * lanes),
            transcendentals=0,
        ),
        name="out",
    )(x, *rows, *hidden, *down)


def stack_kernel(*refs):
    depth = refs[0].shape[0]
    for at, piece in enumerate(refs[:-1]):
        refs[-1][at * depth : (at + 1) * depth, :] = piece[...]


def stack(pieces):
    depth, columns = pieces[0].shape
    block = columns // 2
    return pl.pallas_call(
        stack_kernel,
        grid=(2,),
        in_specs=[pl.BlockSpec((depth, block), lambda j: (0, j))] * 4,
        out_specs=pl.BlockSpec((4 * depth, block), lambda j: (0, j)),
        out_shape=jax.ShapeDtypeStruct((4 * depth, columns), jnp.bfloat16),
        compiler_params=pltpu.CompilerParams(vmem_limit_bytes=VMEM_LIMIT),
        name="stack",
    )(*pieces)


def regroup_kernel(x_ref, *refs):
    tails, pieces, outs = refs[:2], refs[2:6], refs[6:]
    pair, columns = pieces[0].shape
    capacity = pair // 2
    for direction, out in enumerate(outs):
        part = slice(direction * capacity, (direction + 1) * capacity)
        for offset, piece in zip(OFFSETS, pieces):
            start = pl.multiple_of(lax.rem(x_ref[0] - offset + RING, RING) * columns, 128)
            out[:, pl.ds(start, columns)] = piece[part, :]
        out[:, RING * columns :] = tails[direction][...]


def regroup(x, rows, pieces):
    pair, columns = pieces[0].shape
    wide = RING * columns + 128
    whole = pl.BlockSpec((pair, columns), lambda j, x: (0, 0))
    return pl.pallas_call(
        regroup_kernel,
        grid_spec=pltpu.PrefetchScalarGridSpec(
            num_scalar_prefetch=1,
            grid=(1,),
            in_specs=[pl.BlockSpec((pair // 2, 128), lambda j, x: (0, RING * columns // 128))] * 2
            + [whole] * 4,
            out_specs=[pl.BlockSpec((pair // 2, wide), lambda j, x: (0, 0))] * 2,
        ),
        out_shape=[jax.ShapeDtypeStruct((pair // 2, wide), jnp.bfloat16)] * 2,
        compiler_params=pltpu.CompilerParams(vmem_limit_bytes=VMEM_LIMIT),
        name="regroup",
    )(x, *rows, *pieces)


def merge_kernel(*refs):
    pieces, outs = refs[:-2], refs[-2:]
    count, width = outs[0].shape
    token = lax.broadcasted_iota(jnp.int32, (count, count), 1).astype(jnp.float32)
    for direction, out in enumerate(outs):
        mine = pieces[direction::2]
        rows = jnp.concatenate([piece[:, :width] for piece in mine], axis=0)
        place = jnp.concatenate([piece[:, width:] for piece in mine], axis=0).astype(jnp.float32)
        pick = jnp.where(place[:, 3:4] == token, 1.0, 0.0).astype(jnp.bfloat16)
        out[...] = lax.dot_general(
            pick, rows, (((0,), (0,)), ((), ())), preferred_element_type=jnp.float32
        ).astype(jnp.bfloat16)


def merge(pieces):
    count = sum(piece.shape[0] for piece in pieces) // 2
    whole = pl.BlockSpec(memory_space=pltpu.VMEM)
    shape = jax.ShapeDtypeStruct((count, pieces[0].shape[1] - 128), jnp.bfloat16)
    return pl.pallas_call(
        merge_kernel,
        in_specs=[whole] * len(pieces),
        out_specs=[whole] * 2,
        out_shape=[shape] * 2,
        compiler_params=pltpu.CompilerParams(vmem_limit_bytes=VMEM_LIMIT),
        name="merge",
    )(*pieces)


def after(values, deps):
    return lax.optimization_barrier((tuple(values), tuple(deps)))[0]


def per_device(
    forward_states,
    reverse_states,
    forward_routes,
    reverse_routes,
    forward_share,
    reverse_share,
    layer_gate,
    layer_up,
    layer_down,
):
    pipes = lax.axis_size("pipe")
    send = functools.partial(move, pipes=pipes)
    mine = lax.axis_index("ep").astype(jnp.int32)
    z = mine // (RING * CORES)
    x = (mine // CORES) % RING
    count, width = forward_states.shape[1:]
    columns = width // RING
    gate, up, down = layer_gate[0], layer_up[0], layer_down[0]

    at_x = x[None]

    def spread(h):
        return [h] + [send(h, steps=-o) for o in OFFSETS[1:]]

    def back(outs, flip):
        return [
            send(out, steps=o, flip=flip) if flip or o else out for out, o in zip(outs, OFFSETS)
        ]

    def first(f, r):
        return send(f, steps=1), send(r, steps=-1)

    def second(f, r):
        return send(r, steps=1), send(f, steps=-1)

    with jax.named_scope("weights"):
        weights = [gate, send(gate, core=True), up, send(up, core=True)]

    with jax.named_scope("pack"):
        own_f, own_r, oth = pack(
            jnp.stack([mine, z]),
            forward_routes.reshape(1, -1),
            reverse_routes.reshape(1, -1),
            forward_share.reshape(1, count),
            reverse_share.reshape(1, count),
            forward_states[0],
            reverse_states[0],
        )
    half = count // 2
    oth_f, oth_r = oth[:half], oth[half:]
    with jax.named_scope("swap"):
        swapped = send(oth, flip=True)
    with jax.named_scope("first1"):
        own_left_f, own_right_r = first(own_f, own_r)

    with jax.named_scope("down"):
        parts = list(slices(after((at_x,), (own_f,))[0], down))
        parts[1:3] = after(parts[1:3], (weights[1], weights[3]))
        parts[1:3] = [send(part, steps=-o) for part, o in zip(parts[1:3], OFFSETS[1:3])]

    with jax.named_scope("far1"):
        own_left_f, own_right_r, swapped, *_ = after(
            (own_left_f, own_right_r, swapped), parts[1:3]
        )
        far_f, far_r = first(own_left_f, own_right_r)
    with jax.named_scope("second1"):
        left_r, right_f = second(*after((own_f, own_r), (own_left_f, own_right_r)))
    rows1 = [own_f, own_r, own_left_f, left_r, right_f, own_right_r, far_f, far_r]
    with jax.named_scope("down"):
        parts[3:] = after(parts[3:], rows1)
        parts[3] = send(parts[3], steps=-OFFSETS[3])
    with jax.named_scope("hidden1"):
        hidden1 = spread(hidden_rows(rows1, weights))
    with jax.named_scope("down"):
        half_down = stack(after(parts, hidden1[:1]))
        down = [half_down, send(half_down, core=True)]
    with jax.named_scope("first0"):
        (swapped,) = after((swapped,), parts[3:] + hidden1[1:])
        f, r = swapped[:half], swapped[half:]
        left_f, right_r = first(f, r)
    with jax.named_scope("out1"):
        outs1 = out_rows(at_x, rows1, hidden1, down)
    with jax.named_scope("back1"):
        back1 = back(outs1, False)
    with jax.named_scope("far0"):
        far_f, far_r = first(*after((left_f, right_r), outs1))
    with jax.named_scope("second0"):
        left_r, right_f = second(*after((f, r), back1))
    rows0 = [f, r, left_f, left_r, right_f, right_r, far_f, far_r]
    with jax.named_scope("relay1"):
        whole_f, whole_r = regroup(at_x, (own_f, own_r), back1)
        sent1 = [send(whole_f, by=1), send(whole_r, by=-1)]
    with jax.named_scope("hidden0"):
        hidden0 = spread(hidden_rows(after(rows0, (whole_f, whole_r)), weights))
    with jax.named_scope("out0"):
        outs0 = out_rows(at_x, rows0, after(hidden0, sent1), down)
    with jax.named_scope("back0"):
        back0 = back(outs0, True)
    with jax.named_scope("relay0"):
        whole_f, whole_r = regroup(at_x, (oth_f, oth_r), back0)
        sent0 = [send(whole_f, by=1), send(whole_r, by=-1)]
    with jax.named_scope("merge"):
        ahead, behind = merge(sent1 + sent0)
    return (ahead[None], behind[None])


def solution(mesh):
    in_specs = (
        P("pipe", "ep", None),
        P("pipe", "ep", None),
        P(None, "pipe", None, None),
        P(None, "pipe", None, None),
        P(None, "pipe", "ep"),
        P(None, "pipe", "ep"),
        P("pipe", None, "ep"),
        P("pipe", None, "ep"),
        P("pipe", "ep", None),
    )
    out_specs = (P("pipe", "ep", None), P("pipe", "ep", None))
    return jax.shard_map(
        per_device, mesh=mesh, in_specs=in_specs, out_specs=out_specs, check_vma=False
    )
```

time: 550 us -> 181 us (0.33)
  the two profiles are of different devices: /device:TPU:31 before, /device:TPU:10 now
where the time goes in v1:
time: 181 us; the launch traced here: 179 us
  waiting for transfers between devices  92.1 us (51%)
  starting transfers between devices  63.7 us (35%)
  Pallas kernels  19.4 us (11%)
  local copies, waits for them, and re-layouts  2.46 us (1%)
    ppermute x36, waiting for transfers between devices, move(): return lax.ppermute(shard, ('pipe', 'ep'), pairs)  92.1 us
    ppermute x36, starting transfers between devices, move(): return lax.ppermute(shard, ('pipe', 'ep'), pairs)  63.7 us
    pallas_call x2, Pallas kernels, hidden_rows(): pl.pallas_call(functools.partial(hidden_kernel, 7), in_specs=[whole] * (l...  8.41 us
  transfers between devices with their start and end apart: 36, of which 24 were waited for; matrix products, arithmetic and copies ran while one was open for 1% of the time, Pallas kernels for 9%

profile of v1, /device:TPU:10, one launch (start us, length us, event | category | flops | bytes accessed | tf_op | source)
XLA Modules:
  0.0 178.5 jit_solution(15761637045441134309)
XLA Ops:
  1.3 3.6 %pack.1 = (bf16[32,7296]{1,0:T(8,128)(2,1)S(1)}, bf16[32,7296]{1,0:T(8,128)(2,1)S(1)}, bf16[64,7296]{1,0:T(8,128)(2,1)}) custom-call(s32[2]{0:T(128)S(1)} %pad_add_fusion.place, s32[1,1024]{1,0:T(1,128)} %bitcast.23, s32[1,1024]{1,0:T(1,128)} %bitcast.24, f32[1,64]{1,0:T(1,128)} %bitcast.25, f32[1,64]{1,0:T(1,128)} %bitcast.26, bf16[64,7168]{1,0:T(8,128)(2,1)} %bitcast.21, ...), custom_call_target="tpu_custom_call" | custom-call | tf_op jit(solution)/shard_map/pack/pack/pallas_call | solution.py:131
  12.7 7.8 %collective-permute-done.refs_2_ = bf16[32,7296]{1,0:T(8,128)(2,1)S(1)} collective-permute-done((bf16[32,7296]{1,0:T(8,128)(2,1)S(1)}, bf16[32,7296]{1,0:T(8,128)(2,1)S(1)}, u32[]{:S(2)}, u32[]{:S(2)}) %collective-permute-start) | collective-permute-done | bytes 466976 | tf_op jit(solution)/shard_map/first1/ppermute | solution.py:33
  22.1 6.1 %collective-permute-done.2 = bf16[64,7296]{1,0:T(8,128)(2,1)} collective-permute-done((bf16[64,7296]{1,0:T(8,128)(2,1)}, bf16[64,7296]{1,0:T(8,128)(2,1)}, u32[]{:S(2)}, u32[]{:S(2)}) %collective-permute-start.2) | collective-permute-done | bytes 933920 | tf_op jit(solution)/shard_map/swap/ppermute | solution.py:33
  34.4 9.6 %collective-permute-done.7.refs_3_ = bf16[32,7296]{1,0:T(8,128)(2,1)S(1)} collective-permute-done((bf16[32,7296]{1,0:T(8,128)(2,1)S(1)}, bf16[32,7296]{1,0:T(8,128)(2,1)S(1)}, u32[]{:S(2)}, u32[]{:S(2)}) %collective-permute-start.7) | collective-permute-done | bytes 466976 | tf_op jit(solution)/shard_map/second1/ppermute | solution.py:33
  45.2 6.4 %collective-permute-done.9.refs_6_ = bf16[32,7296]{1,0:T(8,128)(2,1)S(1)} collective-permute-done((bf16[32,7296]{1,0:T(8,128)(2,1)S(1)}, bf16[32,7296]{1,0:T(8,128)(2,1)S(1)}, u32[]{:S(2)}, u32[]{:S(2)}) %collective-permute-start.9) | collective-permute-done | bytes 466976 | tf_op jit(solution)/shard_map/far1/ppermute | solution.py:33
  52.5 2.9 %collective-permute-start.14 = (bf16[128,1792]{1,0:T(8,128)(2,1)S(1)}, bf16[128,1792]{1,0:T(8,128)(2,1)S(1)}, u32[]{:S(2)}, u32[]{:S(2)}) collective-permute-start(bf16[128,1792]{1,0:T(8,128)(2,1)S(1)} %get-tuple-element.67), channel_id=1, source_target_pairs={{0,4},{1,5},{2,6},{3,7},{4,0},{5,1},{6,2},{7,3},{8,12},{9,13},{10,... | collective-permute-start | bytes 1376264 | tf_op jit(solution)/shard_map/down/ppermute | solution.py:33
  55.5 4.3 %hidden.2.refs_8_ = bf16[256,256]{1,0:T(8,128)(2,1)S(1)} custom-call(bf16[32,7296]{1,0:T(8,128)(2,1)S(1)} %get-tuple-element.64.refs_0_, bf16[32,7296]{1,0:T(8,128)(2,1)S(1)} %get-tuple-element.63.refs_1_, bf16[32,7296]{1,0:T(8,128)(2,1)S(1)} %collective-permute-done.refs_2_, bf16[32,7296]{1,0:T(8,128)(2,1)S(1)} %collective-permute-done.7.refs_3_, ...), custom_call_target="tpu_custom_call" | custom-call | flops 1879048192 | bytes 11010048 | tf_op jit(solution)/shard_map/hidden1/hidden/pallas_call | solution.py:172
  62.7 4.1 %collective-permute-done.14.refs_3_ = bf16[128,1792]{1,0:T(8,128)(2,1)S(1)} collective-permute-done((bf16[128,1792]{1,0:T(8,128)(2,1)S(1)}, bf16[128,1792]{1,0:T(8,128)(2,1)S(1)}, u32[]{:S(2)}, u32[]{:S(2)}) %collective-permute-start.14) | collective-permute-done | bytes 458784 | tf_op jit(solution)/shard_map/down/ppermute | solution.py:33
  75.0 3.0 %collective-permute-start.16 = (bf16[64,1792]{1,0:T(8,128)(2,1)S(1)}, bf16[64,1792]{1,0:T(8,128)(2,1)S(1)}, u32[]{:S(2)}, u32[]{:S(2)}) collective-permute-start(bf16[64,1792]{1,0:T(8,128)(2,1)S(1)} %get-tuple-element.73), channel_id=1, source_target_pairs={{0,6},{1,7},{2,0},{3,1},{4,2},{5,3},{6,4},{7,5},{8,14},{9,15},{10,... | collective-permute-start | bytes 688136 | tf_op jit(solution)/shard_map/back1/ppermute | solution.py:33
  78.1 3.5 %collective-permute-start.18 = (bf16[64,1792]{1,0:T(8,128)(2,1)S(1)}, bf16[64,1792]{1,0:T(8,128)(2,1)S(1)}, u32[]{:S(2)}, u32[]{:S(2)}) collective-permute-start(bf16[64,1792]{1,0:T(8,128)(2,1)S(1)} %get-tuple-element.75), channel_id=1, source_target_pairs={{0,4},{1,5},{2,6},{3,7},{4,0},{5,1},{6,2},{7,3},{8,12},{9,13},{10,... | collective-permute-start | bytes 688136 | tf_op jit(solution)/shard_map/back1/ppermute | solution.py:33
  81.6 2.8 %collective-permute-done.21.refs_2_ = bf16[32,7296]{1,0:T(8,128)(2,1)S(1)} collective-permute-done((bf16[32,7296]{1,0:T(8,128)(2,1)S(1)}, bf16[32,7296]{1,0:T(8,128)(2,1)S(1)}, u32[]{:S(2)}, u32[]{:S(2)}) %collective-permute-start.21) | collective-permute-done | bytes 466976 | tf_op jit(solution)/shard_map/first0/ppermute | solution.py:33
  88.7 5.9 %collective-permute-done.16.refs_3_ = bf16[64,1792]{1,0:T(8,128)(2,1)S(1)} collective-permute-done((bf16[64,1792]{1,0:T(8,128)(2,1)S(1)}, bf16[64,1792]{1,0:T(8,128)(2,1)S(1)}, u32[]{:S(2)}, u32[]{:S(2)}) %collective-permute-start.16) | collective-permute-done | bytes 229408 | tf_op jit(solution)/shard_map/back1/ppermute | solution.py:33
  94.6 2.9 %collective-permute-done.18.refs_5_ = bf16[64,1792]{1,0:T(8,128)(2,1)S(1)} collective-permute-done((bf16[64,1792]{1,0:T(8,128)(2,1)S(1)}, bf16[64,1792]{1,0:T(8,128)(2,1)S(1)}, u32[]{:S(2)}, u32[]{:S(2)}) %collective-permute-start.18) | collective-permute-done | bytes 229408 | tf_op jit(solution)/shard_map/back1/ppermute | solution.py:33
  99.6 5.2 %collective-permute-start.19 = (bf16[32,7296]{1,0:T(8,128)(2,1)S(1)}, bf16[32,7296]{1,0:T(8,128)(2,1)S(1)}, u32[]{:S(2)}, u32[]{:S(2)}) collective-permute-start(bf16[32,7296]{1,0:T(8,128)(2,1)S(1)} %get-tuple-element.76), channel_id=1, source_target_pairs={{0,16},{1,17},{2,18},{3,19},{4,20},{5,21},{6,22},{7,23},{8,24},{9,... | collective-permute-start | bytes 1400840 | tf_op jit(solution)/shard_map/relay1/ppermute | solution.py:33
  104.8 6.8 %collective-permute-start.20 = (bf16[32,7296]{1,0:T(8,128)(2,1)S(1)}, bf16[32,7296]{1,0:T(8,128)(2,1)S(1)}, u32[]{:S(2)}, u32[]{:S(2)}) collective-permute-start(bf16[32,7296]{1,0:T(8,128)(2,1)S(1)} %get-tuple-element.77), channel_id=1, source_target_pairs={{16,0},{17,1},{18,2},{19,3},{20,4},{21,5},{22,6},{23,7},{24,8},{25... | collective-permute-start | bytes 1400840 | tf_op jit(solution)/shard_map/relay1/ppermute | solution.py:33
  113.4 4.1 %hidden.3.refs_8_ = bf16[256,256]{1,0:T(8,128)(2,1)S(1)} custom-call(bf16[32,7296]{1,0:T(8,128)(2,1)S(1)} %get-tuple-element.84.refs_0_, bf16[32,7296]{1,0:T(8,128)(2,1)S(1)} %get-tuple-element.85.refs_1_, bf16[32,7296]{1,0:T(8,128)(2,1)S(1)} %collective-permute-done.21.refs_2_, bf16[32,7296]{1,0:T(8,128)(2,1)S(1)} %collective-permute-done.22.refs_3_, ...), custom_call_target="tpu_custom_call" | custom-call | flops 1879048192 | bytes 11010048 | tf_op jit(solution)/shard_map/hidden0/hidden/pallas_call | solution.py:172
  119.7 3.0 %collective-permute-start.29 = (bf16[256,256]{1,0:T(8,128)(2,1)S(1)}, bf16[256,256]{1,0:T(8,128)(2,1)S(1)}, u32[]{:S(2)}, u32[]{:S(2)}) collective-permute-start(bf16[256,256]{1,0:T(8,128)(2,1)S(1)} %hidden.3.refs_8_), channel_id=1, source_target_pairs={{0,4},{1,5},{2,6},{3,7},{4,0},{5,1},{6,2},{7,3},{8,12},{9,13},{10,... | collective-permute-start | bytes 393224 | tf_op jit(solution)/shard_map/hidden0/ppermute | solution.py:33
  132.0 3.9 %collective-permute-start.33 = (bf16[64,1792]{1,0:T(8,128)(2,1)S(1)}, bf16[64,1792]{1,0:T(8,128)(2,1)S(1)}, u32[]{:S(2)}, u32[]{:S(2)}) collective-permute-start(bf16[64,1792]{1,0:T(8,128)(2,1)S(1)} %get-tuple-element.99), channel_id=1, source_target_pairs={{0,12},{1,13},{2,14},{3,15},{4,8},{5,9},{6,10},{7,11},{8,4},{9,5},... | collective-permute-start | bytes 688136 | tf_op jit(solution)/shard_map/back0/ppermute | solution.py:33
  137.2 4.8 %collective-permute-done.31.refs_3_ = bf16[64,1792]{1,0:T(8,128)(2,1)S(1)} collective-permute-done((bf16[64,1792]{1,0:T(8,128)(2,1)S(1)}, bf16[64,1792]{1,0:T(8,128)(2,1)S(1)}, u32[]{:S(2)}, u32[]{:S(2)}) %collective-permute-start.31) | collective-permute-done | bytes 229408 | tf_op jit(solution)/shard_map/back0/ppermute | solution.py:33
  142.0 5.5 %collective-permute-done.32.refs_4_ = bf16[64,1792]{1,0:T(8,128)(2,1)S(1)} collective-permute-done((bf16[64,1792]{1,0:T(8,128)(2,1)S(1)}, bf16[64,1792]{1,0:T(8,128)(2,1)S(1)}, u32[]{:S(2)}, u32[]{:S(2)}) %collective-permute-start.32) | collective-permute-done | bytes 229408 | tf_op jit(solution)/shard_map/back0/ppermute | solution.py:33
  150.0 5.5 %collective-permute-start.34 = (bf16[32,7296]{1,0:T(8,128)(2,1)S(1)}, bf16[32,7296]{1,0:T(8,128)(2,1)S(1)}, u32[]{:S(2)}, u32[]{:S(2)}) collective-permute-start(bf16[32,7296]{1,0:T(8,128)(2,1)S(1)} %get-tuple-element.100), channel_id=1, source_target_pairs={{0,16},{1,17},{2,18},{3,19},{4,20},{5,21},{6,22},{7,23},{8,24},{9,... | collective-permute-start | bytes 1400840 | tf_op jit(solution)/shard_map/relay0/ppermute | solution.py:33
  155.5 3.4 %collective-permute-start.35 = (bf16[32,7296]{1,0:T(8,128)(2,1)S(1)}, bf16[32,7296]{1,0:T(8,128)(2,1)S(1)}, u32[]{:S(2)}, u32[]{:S(2)}) collective-permute-start(bf16[32,7296]{1,0:T(8,128)(2,1)S(1)} %get-tuple-element.101), channel_id=1, source_target_pairs={{16,0},{17,1},{18,2},{19,3},{20,4},{21,5},{22,6},{23,7},{24,8},{25... | collective-permute-start | bytes 1400840 | tf_op jit(solution)/shard_map/relay0/ppermute | solution.py:33
  158.9 14.3 %collective-permute-done.34.refs_2_ = bf16[32,7296]{1,0:T(8,128)(2,1)S(1)} collective-permute-done((bf16[32,7296]{1,0:T(8,128)(2,1)S(1)}, bf16[32,7296]{1,0:T(8,128)(2,1)S(1)}, u32[]{:S(2)}, u32[]{:S(2)}) %collective-permute-start.34) | collective-permute-done | bytes 466976 | tf_op jit(solution)/shard_map/relay0/ppermute | solution.py:33
  173.2 3.6 %collective-permute-done.35.refs_3_ = bf16[32,7296]{1,0:T(8,128)(2,1)S(1)} collective-permute-done((bf16[32,7296]{1,0:T(8,128)(2,1)S(1)}, bf16[32,7296]{1,0:T(8,128)(2,1)S(1)}, u32[]{:S(2)}, u32[]{:S(2)}) %collective-permute-start.35) | collective-permute-done | bytes 466976 | tf_op jit(solution)/shard_map/relay0/ppermute | solution.py:33
  (65 shorter events, 54.6 us)
Async XLA Ops:
  4.9 23.3 %collective-permute-start.2 = (bf16[64,7296]{1,0:T(8,128)(2,1)}, bf16[64,7296]{1,0:T(8,128)(2,1)}, u32[]{:S(2)}, u32[]{:S(2)}) collective-permute-start(bf16[64,7296]{1,0:T(8,128)(2,1)} %get-tuple-element.55), channel_id=1, source_target_pairs={{0,8},{1,9},{2,10},{3,11},{4,12},{5,13},{6,14},{7,15},{8,0},{9,1},... | collective-permute-start | bytes 2801672 | tf_op jit(solution)/shard_map/swap/ppermute | solution.py:33
  8.4 13.7 %collective-permute-start.1 = (bf16[32,7296]{1,0:T(8,128)(2,1)S(1)}, bf16[32,7296]{1,0:T(8,128)(2,1)}, u32[]{:S(2)}, u32[]{:S(2)}) collective-permute-start(bf16[32,7296]{1,0:T(8,128)(2,1)S(1)} %get-tuple-element.63.refs_1_), channel_id=1, source_target_pairs={{0,6},{1,7},{2,0},{3,1},{4,2},{5,3},{6,4},{7,5},{8,14},{9,15},{10,... | collective-permute-start | bytes 1400840 | tf_op jit(solution)/shard_map/first1/ppermute | solution.py:33
  10.6 18.6 %collective-permute-start.5 = (bf16[128,1792]{1,0:T(8,128)(2,1)S(1)}, bf16[128,1792]{1,0:T(8,128)(2,1)S(1)}, u32[]{:S(2)}, u32[]{:S(2)}) collective-permute-start(bf16[128,1792]{1,0:T(8,128)(2,1)S(1)} %get-tuple-element.59), channel_id=1, source_target_pairs={{0,2},{1,3},{2,4},{3,5},{4,6},{5,7},{6,0},{7,1},{8,10},{9,11},{10,... | collective-permute-start | bytes 1376264 | tf_op jit(solution)/shard_map/down/ppermute | solution.py:33
  12.1 18.2 %collective-permute-start.6 = (bf16[128,1792]{1,0:T(8,128)(2,1)S(1)}, bf16[128,1792]{1,0:T(8,128)(2,1)S(1)}, u32[]{:S(2)}, u32[]{:S(2)}) collective-permute-start(bf16[128,1792]{1,0:T(8,128)(2,1)S(1)} %get-tuple-element.60), channel_id=1, source_target_pairs={{0,6},{1,7},{2,0},{3,1},{4,2},{5,3},{6,4},{7,5},{8,14},{9,15},{10,... | collective-permute-start | bytes 1376264 | tf_op jit(solution)/shard_map/down/ppermute | solution.py:33
  30.4 13.6 %collective-permute-start.7 = (bf16[32,7296]{1,0:T(8,128)(2,1)S(1)}, bf16[32,7296]{1,0:T(8,128)(2,1)S(1)}, u32[]{:S(2)}, u32[]{:S(2)}) collective-permute-start(bf16[32,7296]{1,0:T(8,128)(2,1)S(1)} %get-tuple-element.63.refs_1_), channel_id=1, source_target_pairs={{0,2},{1,3},{2,4},{3,5},{4,6},{5,7},{6,0},{7,1},{8,10},{9,11},{10,... | collective-permute-start | bytes 1400840 | tf_op jit(solution)/shard_map/second1/ppermute | solution.py:33
  31.6 13.6 %collective-permute-start.8 = (bf16[32,7296]{1,0:T(8,128)(2,1)S(1)}, bf16[32,7296]{1,0:T(8,128)(2,1)S(1)}, u32[]{:S(2)}, u32[]{:S(2)}) collective-permute-start(bf16[32,7296]{1,0:T(8,128)(2,1)S(1)} %get-tuple-element.64.refs_0_), channel_id=1, source_target_pairs={{0,6},{1,7},{2,0},{3,1},{4,2},{5,3},{6,4},{7,5},{8,14},{9,15},{10,... | collective-permute-start | bytes 1400840 | tf_op jit(solution)/shard_map/second1/ppermute | solution.py:33
  32.4 19.2 %collective-permute-start.9 = (bf16[32,7296]{1,0:T(8,128)(2,1)S(1)}, bf16[32,7296]{1,0:T(8,128)(2,1)S(1)}, u32[]{:S(2)}, u32[]{:S(2)}) collective-permute-start(bf16[32,7296]{1,0:T(8,128)(2,1)S(1)} %collective-permute-done.refs_2_), channel_id=1, source_target_pairs={{0,2},{1,3},{2,4},{3,5},{4,6},{5,7},{6,0},{7,1},{8,10},{9,11},{10,... | collective-permute-start | bytes 1400840 | tf_op jit(solution)/shard_map/far1/ppermute | solution.py:33
  33.6 18.9 %collective-permute-start.10 = (bf16[32,7296]{1,0:T(8,128)(2,1)}, bf16[32,7296]{1,0:T(8,128)(2,1)S(1)}, u32[]{:S(2)}, u32[]{:S(2)}) collective-permute-start(bf16[32,7296]{1,0:T(8,128)(2,1)} %collective-permute-done.1.refs_5_), channel_id=1, source_target_pairs={{0,6},{1,7},{2,0},{3,1},{4,2},{5,3},{6,4},{7,5},{8,14},{9,15},{10,... | collective-permute-start | bytes 1400840 | tf_op jit(solution)/shard_map/far1/ppermute | solution.py:33
  52.5 14.2 %collective-permute-start.14 = (bf16[128,1792]{1,0:T(8,128)(2,1)S(1)}, bf16[128,1792]{1,0:T(8,128)(2,1)S(1)}, u32[]{:S(2)}, u32[]{:S(2)}) collective-permute-start(bf16[128,1792]{1,0:T(8,128)(2,1)S(1)} %get-tuple-element.67), channel_id=1, source_target_pairs={{0,4},{1,5},{2,6},{3,7},{4,0},{5,1},{6,2},{7,3},{8,12},{9,13},{10,... | collective-permute-start | bytes 1376264 | tf_op jit(solution)/shard_map/down/ppermute | solution.py:33
  70.7 13.7 %collective-permute-start.21 = (bf16[32,7296]{1,0:T(8,128)(2,1)S(1)}, bf16[32,7296]{1,0:T(8,128)(2,1)S(1)}, u32[]{:S(2)}, u32[]{:S(2)}) collective-permute-start(bf16[32,7296]{1,0:T(8,128)(2,1)S(1)} %get-tuple-element.84.refs_0_), channel_id=1, source_target_pairs={{0,2},{1,3},{2,4},{3,5},{4,6},{5,7},{6,0},{7,1},{8,10},{9,11},{10,... | collective-permute-start | bytes 1400840 | tf_op jit(solution)/shard_map/first0/ppermute | solution.py:33
  72.5 13.7 %collective-permute-start.24 = (bf16[32,7296]{1,0:T(8,128)(2,1)S(1)}, bf16[32,7296]{1,0:T(8,128)(2,1)S(1)}, u32[]{:S(2)}, u32[]{:S(2)}) collective-permute-start(bf16[32,7296]{1,0:T(8,128)(2,1)S(1)} %get-tuple-element.85.refs_1_), channel_id=1, source_target_pairs={{0,6},{1,7},{2,0},{3,1},{4,2},{5,3},{6,4},{7,5},{8,14},{9,15},{10,... | collective-permute-start | bytes 1400840 | tf_op jit(solution)/shard_map/first0/ppermute | solution.py:33
  75.0 19.6 %collective-permute-start.16 = (bf16[64,1792]{1,0:T(8,128)(2,1)S(1)}, bf16[64,1792]{1,0:T(8,128)(2,1)S(1)}, u32[]{:S(2)}, u32[]{:S(2)}) collective-permute-start(bf16[64,1792]{1,0:T(8,128)(2,1)S(1)} %get-tuple-element.73), channel_id=1, source_target_pairs={{0,6},{1,7},{2,0},{3,1},{4,2},{5,3},{6,4},{7,5},{8,14},{9,15},{10,... | collective-permute-start | bytes 688136 | tf_op jit(solution)/shard_map/back1/ppermute | solution.py:33
  78.1 16.5 %collective-permute-start.17 = (bf16[64,1792]{1,0:T(8,128)(2,1)S(1)}, bf16[64,1792]{1,0:T(8,128)(2,1)S(1)}, u32[]{:S(2)}, u32[]{:S(2)}) collective-permute-start(bf16[64,1792]{1,0:T(8,128)(2,1)S(1)} %get-tuple-element.74), channel_id=1, source_target_pairs={{0,2},{1,3},{2,4},{3,5},{4,6},{5,7},{6,0},{7,1},{8,10},{9,11},{10,... | collective-permute-start | bytes 688136 | tf_op jit(solution)/shard_map/back1/ppermute | solution.py:33
  78.1 19.5 %collective-permute-start.18 = (bf16[64,1792]{1,0:T(8,128)(2,1)S(1)}, bf16[64,1792]{1,0:T(8,128)(2,1)S(1)}, u32[]{:S(2)}, u32[]{:S(2)}) collective-permute-start(bf16[64,1792]{1,0:T(8,128)(2,1)S(1)} %get-tuple-element.75), channel_id=1, source_target_pairs={{0,4},{1,5},{2,6},{3,7},{4,0},{5,1},{6,2},{7,3},{8,12},{9,13},{10,... | collective-permute-start | bytes 688136 | tf_op jit(solution)/shard_map/back1/ppermute | solution.py:33
  86.2 18.6 %collective-permute-start.25 = (bf16[32,7296]{1,0:T(8,128)(2,1)S(1)}, bf16[32,7296]{1,0:T(8,128)(2,1)S(1)}, u32[]{:S(2)}, u32[]{:S(2)}) collective-permute-start(bf16[32,7296]{1,0:T(8,128)(2,1)S(1)} %collective-permute-done.21.refs_2_), channel_id=1, source_target_pairs={{0,2},{1,3},{2,4},{3,5},{4,6},{5,7},{6,0},{7,1},{8,10},{9,11},{10,... | collective-permute-start | bytes 1400840 | tf_op jit(solution)/shard_map/far0/ppermute | solution.py:33
  88.2 23.4 %collective-permute-start.26 = (bf16[32,7296]{1,0:T(8,128)(2,1)S(1)}, bf16[32,7296]{1,0:T(8,128)(2,1)S(1)}, u32[]{:S(2)}, u32[]{:S(2)}) collective-permute-start(bf16[32,7296]{1,0:T(8,128)(2,1)S(1)} %collective-permute-done.24.refs_5_), channel_id=1, source_target_pairs={{0,6},{1,7},{2,0},{3,1},{4,2},{5,3},{6,4},{7,5},{8,14},{9,15},{10,... | collective-permute-start | bytes 1400840 | tf_op jit(solution)/shard_map/far0/ppermute | solution.py:33
  97.5 14.2 %collective-permute-start.22 = (bf16[32,7296]{1,0:T(8,128)(2,1)S(1)}, bf16[32,7296]{1,0:T(8,128)(2,1)S(1)}, u32[]{:S(2)}, u32[]{:S(2)}) collective-permute-start(bf16[32,7296]{1,0:T(8,128)(2,1)S(1)} %get-tuple-element.85.refs_1_), channel_id=1, source_target_pairs={{0,2},{1,3},{2,4},{3,5},{4,6},{5,7},{6,0},{7,1},{8,10},{9,11},{10,... | collective-permute-start | bytes 1400840 | tf_op jit(solution)/shard_map/second0/ppermute | solution.py:33
  97.5 15.9 %collective-permute-start.23 = (bf16[32,7296]{1,0:T(8,128)(2,1)S(1)}, bf16[32,7296]{1,0:T(8,128)(2,1)S(1)}, u32[]{:S(2)}, u32[]{:S(2)}) collective-permute-start(bf16[32,7296]{1,0:T(8,128)(2,1)S(1)} %get-tuple-element.84.refs_0_), channel_id=1, source_target_pairs={{0,6},{1,7},{2,0},{3,1},{4,2},{5,3},{6,4},{7,5},{8,14},{9,15},{10,... | collective-permute-start | bytes 1400840 | tf_op jit(solution)/shard_map/second0/ppermute | solution.py:33
  99.6 23.0 %collective-permute-start.19 = (bf16[32,7296]{1,0:T(8,128)(2,1)S(1)}, bf16[32,7296]{1,0:T(8,128)(2,1)S(1)}, u32[]{:S(2)}, u32[]{:S(2)}) collective-permute-start(bf16[32,7296]{1,0:T(8,128)(2,1)S(1)} %get-tuple-element.76), channel_id=1, source_target_pairs={{0,16},{1,17},{2,18},{3,19},{4,20},{5,21},{6,22},{7,23},{8,24},{9,... | collective-permute-start | bytes 1400840 | tf_op jit(solution)/shard_map/relay1/ppermute | solution.py:33
  104.8 20.4 %collective-permute-start.20 = (bf16[32,7296]{1,0:T(8,128)(2,1)S(1)}, bf16[32,7296]{1,0:T(8,128)(2,1)S(1)}, u32[]{:S(2)}, u32[]{:S(2)}) collective-permute-start(bf16[32,7296]{1,0:T(8,128)(2,1)S(1)} %get-tuple-element.77), channel_id=1, source_target_pairs={{16,0},{17,1},{18,2},{19,3},{20,4},{21,5},{22,6},{23,7},{24,8},{25... | collective-permute-start | bytes 1400840 | tf_op jit(solution)/shard_map/relay1/ppermute | solution.py:33
  131.2 16.3 %collective-permute-start.32 = (bf16[64,1792]{1,0:T(8,128)(2,1)S(1)}, bf16[64,1792]{1,0:T(8,128)(2,1)S(1)}, u32[]{:S(2)}, u32[]{:S(2)}) collective-permute-start(bf16[64,1792]{1,0:T(8,128)(2,1)S(1)} %get-tuple-element.98), channel_id=1, source_target_pairs={{0,10},{1,11},{2,12},{3,13},{4,14},{5,15},{6,8},{7,9},{8,2},{9,3},... | collective-permute-start | bytes 688136 | tf_op jit(solution)/shard_map/back0/ppermute | solution.py:33
  132.0 17.9 %collective-permute-start.33 = (bf16[64,1792]{1,0:T(8,128)(2,1)S(1)}, bf16[64,1792]{1,0:T(8,128)(2,1)S(1)}, u32[]{:S(2)}, u32[]{:S(2)}) collective-permute-start(bf16[64,1792]{1,0:T(8,128)(2,1)S(1)} %get-tuple-element.99), channel_id=1, source_target_pairs={{0,12},{1,13},{2,14},{3,15},{4,8},{5,9},{6,10},{7,11},{8,4},{9,5},... | collective-permute-start | bytes 688136 | tf_op jit(solution)/shard_map/back0/ppermute | solution.py:33
  150.0 23.2 %collective-permute-start.34 = (bf16[32,7296]{1,0:T(8,128)(2,1)S(1)}, bf16[32,7296]{1,0:T(8,128)(2,1)S(1)}, u32[]{:S(2)}, u32[]{:S(2)}) collective-permute-start(bf16[32,7296]{1,0:T(8,128)(2,1)S(1)} %get-tuple-element.100), channel_id=1, source_target_pairs={{0,16},{1,17},{2,18},{3,19},{4,20},{5,21},{6,22},{7,23},{8,24},{9,... | collective-permute-start | bytes 1400840 | tf_op jit(solution)/shard_map/relay0/ppermute | solution.py:33
  155.5 21.2 %collective-permute-start.35 = (bf16[32,7296]{1,0:T(8,128)(2,1)S(1)}, bf16[32,7296]{1,0:T(8,128)(2,1)S(1)}, u32[]{:S(2)}, u32[]{:S(2)}) collective-permute-start(bf16[32,7296]{1,0:T(8,128)(2,1)S(1)} %get-tuple-element.101), channel_id=1, source_target_pairs={{16,0},{17,1},{18,2},{19,3},{20,4},{21,5},{22,6},{23,7},{24,8},{25... | collective-permute-start | bytes 1400840 | tf_op jit(solution)/shard_map/relay0/ppermute | solution.py:33
  (14 other events, 207.2 us)

commit v2 on v1

--- a/solution.py
+++ b/solution.py
@@ -146,13 +146,17 @@
     )(place, *[pltpu.with_memory_space_constraint(a, pltpu.HBM) for a in arrays])
 
 
-def hidden_kernel(steps, *refs):
+def planned(refs, plan, lanes):
+    return jnp.concatenate([refs[a][start : start + n, lanes] for a, start, n in plan], axis=0)
+
+
+def hidden_kernel(steps, plan, *refs):
     rows, (go, gt, uo, ut), (out, gated, upward) = refs[:-7], refs[-7:-3], refs[-3:]
     block = go.shape[0] // steps
 
     def step(at, _):
         part = pl.ds(pl.multiple_of(at * block, 128), block)
-        x = jnp.concatenate([r[:, part] for r in rows], axis=0)
+        x = planned(rows, plan, part)
         g = jnp.concatenate([go[part, :], gt[part, :]], axis=1)
         u = jnp.concatenate([uo[part, :], ut[part, :]], axis=1)
         gated[...] += jnp.dot(x, g, preferred_element_type=jnp.float32)
@@ -165,12 +169,12 @@
     out[...] = (jax.nn.silu(gated[...]) * upward[...]).astype(jnp.bfloat16)
 
 
-def hidden_rows(rows, weights):
+def hidden_rows(rows, plan, weights):
     width, lanes = weights[0].shape
-    count = sum(r.shape[0] for r in rows)
+    count = sum(n for _, _, n in plan)
     whole = pl.BlockSpec(memory_space=pltpu.VMEM)
     return pl.pallas_call(
-        functools.partial(hidden_kernel, 7),
+        functools.partial(hidden_kernel, 7, plan),
         in_specs=[whole] * (len(rows) + 4),
         out_specs=whole,
         out_shape=jax.ShapeDtypeStruct((count, 2 * lanes), jnp.bfloat16),
@@ -185,9 +189,9 @@
     )(*rows, *weights)
 
 
-def out_kernel(steps, x_ref, *refs):
-    rows, hidden, down, outs, h = refs[:8], refs[8:12], refs[12:14], refs[14:18], refs[18]
-    pair = 2 * rows[0].shape[0]
+def out_kernel(steps, plan, x_ref, *refs):
+    rows, hidden, down, outs, h = refs[:-11], refs[-11:-7], refs[-7:-5], refs[-5:-1], refs[-1]
+    pair = outs[0].shape[0]
     lanes = hidden[0].shape[1] // 2
     columns = down[0].shape[1]
     width = RING * columns
@@ -200,7 +204,7 @@
                     at * pair : (at + 1) * pair,
                     (core * RING + index) * lanes : (core * RING + index + 1) * lanes,
                 ] = source[place * pair : (place + 1) * pair, core * lanes : (core + 1) * lanes]
-    terms = jnp.concatenate([r[:, width:] for r in rows], axis=0).astype(jnp.float32)
+    terms = planned(rows, plan, slice(width, None)).astype(jnp.float32)
     share = terms[:, 0:1] + terms[:, 1:2] + terms[:, 2:3]
 
     def step(j, _):
@@ -208,7 +212,7 @@
         there = pl.ds(pl.multiple_of(x_ref[0] * columns + j * block, 128), block)
         d = jnp.concatenate([r[:, part] for r in down], axis=0)
         branch = jnp.dot(h[...], d, preferred_element_type=jnp.float32)
-        states = jnp.concatenate([r[:, there] for r in rows], axis=0).astype(jnp.float32)
+        states = planned(rows, plan, there).astype(jnp.float32)
         result = (states + share * branch).astype(jnp.bfloat16)
         for at, out in enumerate(outs):
             out[:, part] = result[at * pair : (at + 1) * pair]
@@ -217,16 +221,16 @@
     lax.fori_loop(0, steps, step, 0, unroll=True)
 
 
-def out_rows(x, rows, hidden, down):
-    half, wide = rows[0].shape
-    pair = 2 * half
-    count = RING * pair
+def out_rows(x, rows, plan, hidden, down):
+    wide = rows[0].shape[1]
+    count = sum(n for _, _, n in plan)
+    pair = count // RING
     columns = (wide - 128) // RING
     lanes = hidden[0].shape[1]
     whole = pl.BlockSpec(memory_space=pltpu.VMEM)
     return pl.pallas_call(
-        functools.partial(out_kernel, 7),
-        in_specs=[pl.BlockSpec(memory_space=pltpu.SMEM)] + [whole] * 14,
+        functools.partial(out_kernel, 7, plan),
+        in_specs=[pl.BlockSpec(memory_space=pltpu.SMEM)] + [whole] * (len(rows) + 6),
         out_specs=[whole] * 4,
         out_shape=[jax.ShapeDtypeStruct((pair, columns), jnp.bfloat16)] * 4,
         scratch_shapes=[pltpu.VMEM((count, RING * lanes), jnp.bfloat16)],
@@ -260,8 +264,28 @@
     )(*pieces)
 
 
+def pairs_kernel(a, b, c, d, ab, cd):
+    half = a.shape[0]
+    ab[:half], ab[half:] = a[...], b[...]
+    cd[:half], cd[half:] = c[...], d[...]
+
+
+def pairs(*arrays):
+    half, wide = arrays[0].shape
+    whole = pl.BlockSpec(memory_space=pltpu.VMEM)
+    return pl.pallas_call(
+        pairs_kernel,
+        in_specs=[whole] * 4,
+        out_specs=[whole] * 2,
+        out_shape=[jax.ShapeDtypeStruct((2 * half, wide), arrays[0].dtype)] * 2,
+        compiler_params=pltpu.CompilerParams(vmem_limit_bytes=VMEM_LIMIT),
+        name="pairs",
+    )(*arrays)
+
+
 def regroup_kernel(x_ref, *refs):
-    tails, pieces, outs = refs[:2], refs[2:6], refs[6:]
+    tails, pieces, outs = refs[:-6], refs[-6:-2], refs[-2:]
+    tails = jnp.concatenate([tail[...] for tail in tails], axis=0)
     pair, columns = pieces[0].shape
     capacity = pair // 2
     for direction, out in enumerate(outs):
@@ -269,7 +293,7 @@
         for offset, piece in zip(OFFSETS, pieces):
             start = pl.multiple_of(lax.rem(x_ref[0] - offset + RING, RING) * columns, 128)
             out[:, pl.ds(start, columns)] = piece[part, :]
-        out[:, RING * columns :] = tails[direction][...]
+        out[:, RING * columns :] = tails[part]
 
 
 def regroup(x, rows, pieces):
@@ -281,7 +305,10 @@
         grid_spec=pltpu.PrefetchScalarGridSpec(
             num_scalar_prefetch=1,
             grid=(1,),
-            in_specs=[pl.BlockSpec((pair // 2, 128), lambda j, x: (0, RING * columns // 128))] * 2
+            in_specs=[
+                pl.BlockSpec((r.shape[0], 128), lambda j, x: (0, RING * columns // 128))
+                for r in rows
+            ]
             + [whole] * 4,
             out_specs=[pl.BlockSpec((pair // 2, wide), lambda j, x: (0, 0))] * 2,
         ),
@@ -348,16 +375,11 @@
     def spread(h):
         return [h] + [send(h, steps=-o) for o in OFFSETS[1:]]
 
-    def back(outs, flip):
-        return [
-            send(out, steps=o, flip=flip) if flip or o else out for out, o in zip(outs, OFFSETS)
-        ]
+    def back(outs):
+        return [outs[0]] + [send(out, steps=o) for out, o in zip(outs[1:], OFFSETS[1:])]
 
     def first(f, r):
         return send(f, steps=1), send(r, steps=-1)
-
-    def second(f, r):
-        return send(r, steps=1), send(f, steps=-1)
 
     with jax.named_scope("weights"):
         weights = [gate, send(gate, core=True), up, send(up, core=True)]
@@ -373,7 +395,6 @@
             reverse_states[0],
         )
     half = count // 2
-    oth_f, oth_r = oth[:half], oth[half:]
     with jax.named_scope("swap"):
         swapped = send(oth, flip=True)
     with jax.named_scope("first1"):
@@ -384,47 +405,50 @@
         parts[1:3] = after(parts[1:3], (weights[1], weights[3]))
         parts[1:3] = [send(part, steps=-o) for part, o in zip(parts[1:3], OFFSETS[1:3])]
 
-    with jax.named_scope("far1"):
-        own_left_f, own_right_r, swapped, *_ = after(
-            (own_left_f, own_right_r, swapped), parts[1:3]
-        )
-        far_f, far_r = first(own_left_f, own_right_r)
+        parts[3:] = after(parts[3:], (own_left_f, own_right_r))
+        parts[3] = send(parts[3], steps=-OFFSETS[3])
+    plan = (
+        *((0, 0, half), (1, 0, half)),
+        *((2, 0, half), (4, half, half)),
+        *((5, half, half), (3, 0, half)),
+        *((4, 0, half), (5, 0, half)),
+    )
+
+    def gather(f, r, left_f, right_r, dep):
+        left_f, right_r = after((left_f, right_r), dep)
+        onward, backward = pairs(left_f, r, right_r, f)
+        onward, backward = send(onward, steps=1), send(backward, steps=-1)
+        return [f, r, left_f, right_r, onward, backward]
+
     with jax.named_scope("second1"):
-        left_r, right_f = second(*after((own_f, own_r), (own_left_f, own_right_r)))
-    rows1 = [own_f, own_r, own_left_f, left_r, right_f, own_right_r, far_f, far_r]
+        rows1 = gather(own_f, own_r, own_left_f, own_right_r, [swapped] + parts[1:3])
     with jax.named_scope("down"):
-        parts[3:] = after(parts[3:], rows1)
-        parts[3] = send(parts[3], steps=-OFFSETS[3])
-    with jax.named_scope("hidden1"):
-        hidden1 = spread(hidden_rows(rows1, weights))
-    with jax.named_scope("down"):
-        half_down = stack(after(parts, hidden1[:1]))
+        half_down = stack(parts)
         down = [half_down, send(half_down, core=True)]
     with jax.named_scope("first0"):
-        (swapped,) = after((swapped,), parts[3:] + hidden1[1:])
+        (swapped,) = after((swapped,), parts[1:])
         f, r = swapped[:half], swapped[half:]
         left_f, right_r = first(f, r)
+    with jax.named_scope("hidden1"):
+        hidden1 = spread(hidden_rows(after(rows1, down[1:]), plan, weights))
+    with jax.named_scope("second0"):
+        rows0 = gather(f, r, left_f, right_r, hidden1[1:])
     with jax.named_scope("out1"):
-        outs1 = out_rows(at_x, rows1, hidden1, down)
+        outs1 = out_rows(at_x, rows1, plan, hidden1, down)
     with jax.named_scope("back1"):
-        back1 = back(outs1, False)
-    with jax.named_scope("far0"):
-        far_f, far_r = first(*after((left_f, right_r), outs1))
-    with jax.named_scope("second0"):
-        left_r, right_f = second(*after((f, r), back1))
-    rows0 = [f, r, left_f, left_r, right_f, right_r, far_f, far_r]
+        back1 = back(outs1)
+    with jax.named_scope("hidden0"):
+        hidden0 = spread(hidden_rows(rows0, plan, weights))
     with jax.named_scope("relay1"):
-        whole_f, whole_r = regroup(at_x, (own_f, own_r), back1)
+        whole_f, whole_r = regroup(at_x, [own_f, own_r], after(back1, hidden0[:1]))
         sent1 = [send(whole_f, by=1), send(whole_r, by=-1)]
-    with jax.named_scope("hidden0"):
-        hidden0 = spread(hidden_rows(after(rows0, (whole_f, whole_r)), weights))
     with jax.named_scope("out0"):
-        outs0 = out_rows(at_x, rows0, after(hidden0, sent1), down)
+        outs0 = out_rows(at_x, rows0, plan, hidden0, down)
     with jax.named_scope("back0"):
-        back0 = back(outs0, True)
+        back0 = back(outs0)
     with jax.named_scope("relay0"):
-        whole_f, whole_r = regroup(at_x, (oth_f, oth_r), back0)
-        sent0 = [send(whole_f, by=1), send(whole_r, by=-1)]
+        whole_f, whole_r = regroup(at_x, [swapped], back0)
+        sent0 = [send(whole_f, by=1, flip=True), send(whole_r, by=-1, flip=True)]
     with jax.named_scope("merge"):
         ahead, behind = merge(sent1 + sent0)
     return (ahead[None], behind[None])

time: 181 us -> 166 us (0.917)
  waiting for transfers between devices: 92.1 us -> 80.4 us
    ppermute x36 -> x31, waiting for transfers between devices: 92.1 us -> 80.4 us  [move(): return lax.ppermute(shard, ('pipe', 'ep'), pairs)]
    ppermute x36 -> x31, starting transfers between devices: 63.7 us -> 62.5 us  [move(): return lax.ppermute(shard, ('pipe', 'ep'), pairs)]
    pallas_call x4 -> x6, Pallas kernels: 11.8 us -> 11.9 us  [the longest x2 7.32 us: hidden_rows(): pl.pallas_call(functools.partial(hidden_kernel, 7, plan), in_specs=[whole...]
  transfers between devices with their start and end apart: 36 -> 31, of which waited for: 24 -> 19; matrix products, arithmetic and copies ran while one was open for 1% -> 1% of each run, Pallas kernels for 9% -> 11%
where the time goes in v2:
time: 166 us; the launch traced here: 165 us
  waiting for transfers between devices  80.4 us (48%)
  starting transfers between devices  62.5 us (38%)
  Pallas kernels  20.1 us (12%)
    ppermute x31, waiting for transfers between devices, move(): return lax.ppermute(shard, ('pipe', 'ep'), pairs)  80.4 us
    ppermute x31, starting transfers between devices, move(): return lax.ppermute(shard, ('pipe', 'ep'), pairs)  62.5 us
    pallas_call x2, Pallas kernels, hidden_rows(): pl.pallas_call(functools.partial(hidden_kernel, 7, plan), in_specs=[whole...  7.32 us
    pallas_call x1, Pallas kernels, pack(): pl.pallas_call(pack_kernel, in_specs=[pl.BlockSpec(memory_space=pltpu.SME...  3.57 us
    pallas_call x2, Pallas kernels, out_rows(): pl.pallas_call(functools.partial(out_kernel, 7, plan), in_specs=[pl.Block...  3.35 us
  transfers between devices with their start and end apart: 31, of which 19 were waited for; matrix products, arithmetic and copies ran while one was open for 1% of the time, Pallas kernels for 11%

profile of v2, /device:TPU:10, one launch (start us, length us, event | category | flops | bytes accessed | tf_op | source)
XLA Modules:
  0.0 165.3 jit_solution(13353957152847029261)
XLA Ops:
  1.3 3.6 %pack.1 = (bf16[32,7296]{1,0:T(8,128)(2,1)S(1)}, bf16[32,7296]{1,0:T(8,128)(2,1)S(1)}, bf16[64,7296]{1,0:T(8,128)(2,1)}) custom-call(s32[2]{0:T(128)S(1)} %pad_add_fusion.place, s32[1,1024]{1,0:T(1,128)} %bitcast.23, s32[1,1024]{1,0:T(1,128)} %bitcast.24, f32[1,64]{1,0:T(1,128)} %bitcast.25, f32[1,64]{1,0:T(1,128)} %bitcast.26, bf16[64,7168]{1,0:T(8,128)(2,1)} %bitcast.21, ...), custom_call_target="tpu_custom_call" | custom-call | tf_op jit(solution)/shard_map/pack/pack/pallas_call | solution.py:131
  12.5 8.0 %collective-permute-done.a.refs_2_ = bf16[32,7296]{1,0:T(8,128)(2,1)S(1)} collective-permute-done((bf16[32,7296]{1,0:T(8,128)(2,1)S(1)}, bf16[32,7296]{1,0:T(8,128)(2,1)S(1)}, u32[]{:S(2)}, u32[]{:S(2)}) %collective-permute-start) | collective-permute-done | bytes 466976 | tf_op jit(solution)/shard_map/first1/ppermute | solution.py:33
  24.4 3.7 %collective-permute-done.2.refs_0_ = bf16[64,7296]{1,0:T(8,128)(2,1)} collective-permute-done((bf16[64,7296]{1,0:T(8,128)(2,1)}, bf16[64,7296]{1,0:T(8,128)(2,1)}, u32[]{:S(2)}, u32[]{:S(2)}) %collective-permute-start.2) | collective-permute-done | bytes 933920 | tf_op jit(solution)/shard_map/swap/ppermute | solution.py:33
  34.2 5.6 %collective-permute-start.8 = (bf16[64,7296]{1,0:T(8,128)(2,1)S(1)}, bf16[64,7296]{1,0:T(8,128)(2,1)S(1)}, u32[]{:S(2)}, u32[]{:S(2)}) collective-permute-start(bf16[64,7296]{1,0:T(8,128)(2,1)S(1)} %get-tuple-element.57), channel_id=1, source_target_pairs={{0,6},{1,7},{2,0},{3,1},{4,2},{5,3},{6,4},{7,5},{8,14},{9,15},{10,... | collective-permute-start | bytes 2801672 | tf_op jit(solution)/shard_map/second1/ppermute | solution.py:33
  39.9 2.5 %collective-permute-done.9.refs_3_ = bf16[128,1792]{1,0:T(8,128)(2,1)S(1)} collective-permute-done((bf16[128,1792]{1,0:T(8,128)(2,1)S(1)}, bf16[128,1792]{1,0:T(8,128)(2,1)S(1)}, u32[]{:S(2)}, u32[]{:S(2)}) %collective-permute-start.9) | collective-permute-done | bytes 458784 | tf_op jit(solution)/shard_map/down/ppermute | solution.py:33
  46.4 15.0 %collective-permute-done.7.refs_4_ = bf16[64,7296]{1,0:T(8,128)(2,1)S(1)} collective-permute-done((bf16[64,7296]{1,0:T(8,128)(2,1)S(1)}, bf16[64,7296]{1,0:T(8,128)(2,1)S(1)}, u32[]{:S(2)}, u32[]{:S(2)}) %collective-permute-start.7) | collective-permute-done | bytes 933920 | tf_op jit(solution)/shard_map/second1/ppermute | solution.py:33
  61.4 3.5 %collective-permute-done.8.refs_5_ = bf16[64,7296]{1,0:T(8,128)(2,1)S(1)} collective-permute-done((bf16[64,7296]{1,0:T(8,128)(2,1)S(1)}, bf16[64,7296]{1,0:T(8,128)(2,1)S(1)}, u32[]{:S(2)}, u32[]{:S(2)}) %collective-permute-start.8) | collective-permute-done | bytes 933920 | tf_op jit(solution)/shard_map/second1/ppermute | solution.py:33
  64.9 3.7 %hidden.2.refs_6_ = bf16[256,256]{1,0:T(8,128)(2,1)S(1)} custom-call(bf16[32,7296]{1,0:T(8,128)(2,1)S(1)} %get-tuple-element.61.d.refs_0_, bf16[32,7296]{1,0:T(8,128)(2,1)S(1)} %get-tuple-element.62.b.refs_1_, bf16[32,7296]{1,0:T(8,128)(2,1)S(1)} %collective-permute-done.a.refs_2_, bf16[32,7296]{1,0:T(8,128)(2,1)} %collective-permute-done.1.c.refs_3_, ...), custom_call_target="tpu_custom_call" | custom-call | flops 1879048192 | bytes 11010048 | tf_op jit(solution)/shard_map/hidden1/hidden/pallas_call | solution.py:176
  70.9 2.6 %collective-permute-start.13 = (bf16[256,256]{1,0:T(8,128)(2,1)S(1)}, bf16[256,256]{1,0:T(8,128)(2,1)S(1)}, u32[]{:S(2)}, u32[]{:S(2)}) collective-permute-start(bf16[256,256]{1,0:T(8,128)(2,1)S(1)} %hidden.2.refs_6_), channel_id=1, source_target_pairs={{0,4},{1,5},{2,6},{3,7},{4,0},{5,1},{6,2},{7,3},{8,12},{9,13},{10,... | collective-permute-start | bytes 393224 | tf_op jit(solution)/shard_map/hidden1/ppermute | solution.py:33
  75.4 2.9 %collective-permute-done.13.refs_9_ = bf16[256,256]{1,0:T(8,128)(2,1)S(1)} collective-permute-done((bf16[256,256]{1,0:T(8,128)(2,1)S(1)}, bf16[256,256]{1,0:T(8,128)(2,1)S(1)}, u32[]{:S(2)}, u32[]{:S(2)}) %collective-permute-start.13) | collective-permute-done | bytes 131104 | tf_op jit(solution)/shard_map/hidden1/ppermute | solution.py:33
  82.8 3.1 %collective-permute-start.14 = (bf16[64,1792]{1,0:T(8,128)(2,1)S(1)}, bf16[64,1792]{1,0:T(8,128)(2,1)S(1)}, u32[]{:S(2)}, u32[]{:S(2)}) collective-permute-start(bf16[64,1792]{1,0:T(8,128)(2,1)S(1)} %get-tuple-element.68), channel_id=1, source_target_pairs={{0,6},{1,7},{2,0},{3,1},{4,2},{5,3},{6,4},{7,5},{8,14},{9,15},{10,... | collective-permute-start | bytes 688136 | tf_op jit(solution)/shard_map/back1/ppermute | solution.py:33
  85.9 10.5 %collective-permute-done.19.refs_4_ = bf16[64,7296]{1,0:T(8,128)(2,1)S(1)} collective-permute-done((bf16[64,7296]{1,0:T(8,128)(2,1)S(1)}, bf16[64,7296]{1,0:T(8,128)(2,1)S(1)}, u32[]{:S(2)}, u32[]{:S(2)}) %collective-permute-start.19) | collective-permute-done | bytes 933920 | tf_op jit(solution)/shard_map/second0/ppermute | solution.py:33
  96.4 5.2 %collective-permute-done.20.refs_5_ = bf16[64,7296]{1,0:T(8,128)(2,1)S(1)} collective-permute-done((bf16[64,7296]{1,0:T(8,128)(2,1)S(1)}, bf16[64,7296]{1,0:T(8,128)(2,1)S(1)}, u32[]{:S(2)}, u32[]{:S(2)}) %collective-permute-start.20) | collective-permute-done | bytes 933920 | tf_op jit(solution)/shard_map/second0/ppermute | solution.py:33
  101.6 3.6 %hidden.3.refs_6_ = bf16[256,256]{1,0:T(8,128)(2,1)S(1)} custom-call(bf16[32,7296]{1,0:T(8,128)(2,1)S(1)} %get-tuple-element.91.d.refs_0_, bf16[32,7296]{1,0:T(8,128)(2,1)S(1)} %get-tuple-element.90.b.refs_1_, bf16[32,7296]{1,0:T(8,128)(2,1)S(1)} %collective-permute-done.17.a.refs_2_, bf16[32,7296]{1,0:T(8,128)(2,1)S(1)} %collective-permute-done.18.c.refs_3_, ...), custom_call_target="tpu_custom_call" | custom-call | flops 1879048192 | bytes 11010048 | tf_op jit(solution)/shard_map/hidden0/hidden/pallas_call | solution.py:176
  111.1 2.9 %collective-permute-start.16 = (bf16[64,1792]{1,0:T(8,128)(2,1)S(1)}, bf16[64,1792]{1,0:T(8,128)(2,1)S(1)}, u32[]{:S(2)}, u32[]{:S(2)}) collective-permute-start(bf16[64,1792]{1,0:T(8,128)(2,1)S(1)} %get-tuple-element.70), channel_id=1, source_target_pairs={{0,4},{1,5},{2,6},{3,7},{4,0},{5,1},{6,2},{7,3},{8,12},{9,13},{10,... | collective-permute-start | bytes 688136 | tf_op jit(solution)/shard_map/back1/ppermute | solution.py:33
  114.0 2.5 %collective-permute-done.25.refs_9_ = bf16[256,256]{1,0:T(8,128)(2,1)S(1)} collective-permute-done((bf16[256,256]{1,0:T(8,128)(2,1)S(1)}, bf16[256,256]{1,0:T(8,128)(2,1)S(1)}, u32[]{:S(2)}, u32[]{:S(2)}) %collective-permute-start.25) | collective-permute-done | bytes 131104 | tf_op jit(solution)/shard_map/hidden0/ppermute | solution.py:33
  119.8 6.4 %collective-permute-start.28 = (bf16[64,1792]{1,0:T(8,128)(2,1)S(1)}, bf16[64,1792]{1,0:T(8,128)(2,1)S(1)}, u32[]{:S(2)}, u32[]{:S(2)}) collective-permute-start(bf16[64,1792]{1,0:T(8,128)(2,1)S(1)} %get-tuple-element.85), channel_id=1, source_target_pairs={{0,4},{1,5},{2,6},{3,7},{4,0},{5,1},{6,2},{7,3},{8,12},{9,13},{10,... | collective-permute-start | bytes 688136 | tf_op jit(solution)/shard_map/back0/ppermute | solution.py:33
  126.2 5.2 %collective-permute-start.21 = (bf16[32,7296]{1,0:T(8,128)(2,1)S(1)}, bf16[32,7296]{1,0:T(8,128)(2,1)S(1)}, u32[]{:S(2)}, u32[]{:S(2)}) collective-permute-start(bf16[32,7296]{1,0:T(8,128)(2,1)S(1)} %get-tuple-element.80), channel_id=1, source_target_pairs={{0,16},{1,17},{2,18},{3,19},{4,20},{5,21},{6,22},{7,23},{8,24},{9,... | collective-permute-start | bytes 1400840 | tf_op jit(solution)/shard_map/relay1/ppermute | solution.py:33
  131.4 3.9 %collective-permute-start.22 = (bf16[32,7296]{1,0:T(8,128)(2,1)S(1)}, bf16[32,7296]{1,0:T(8,128)(2,1)S(1)}, u32[]{:S(2)}, u32[]{:S(2)}) collective-permute-start(bf16[32,7296]{1,0:T(8,128)(2,1)S(1)} %get-tuple-element.81), channel_id=1, source_target_pairs={{16,0},{17,1},{18,2},{19,3},{20,4},{21,5},{22,6},{23,7},{24,8},{25... | collective-permute-start | bytes 1400840 | tf_op jit(solution)/shard_map/relay1/ppermute | solution.py:33
  136.2 3.9 %collective-permute-start.29 = (bf16[32,7296]{1,0:T(8,128)(2,1)S(1)}, bf16[32,7296]{1,0:T(8,128)(2,1)S(1)}, u32[]{:S(2)}, u32[]{:S(2)}) collective-permute-start(bf16[32,7296]{1,0:T(8,128)(2,1)S(1)} %get-tuple-element.86), channel_id=1, source_target_pairs={{0,24},{1,25},{2,26},{3,27},{4,28},{5,29},{6,30},{7,31},{8,16},{9,... | collective-permute-start | bytes 1400840 | tf_op jit(solution)/shard_map/relay0/ppermute | solution.py:33
  140.1 4.0 %collective-permute-start.30 = (bf16[32,7296]{1,0:T(8,128)(2,1)S(1)}, bf16[32,7296]{1,0:T(8,128)(2,1)S(1)}, u32[]{:S(2)}, u32[]{:S(2)}) collective-permute-start(bf16[32,7296]{1,0:T(8,128)(2,1)S(1)} %get-tuple-element.87), channel_id=1, source_target_pairs={{16,8},{17,9},{18,10},{19,11},{20,12},{21,13},{22,14},{23,15},{24,... | collective-permute-start | bytes 1400840 | tf_op jit(solution)/shard_map/relay0/ppermute | solution.py:33
  144.1 5.8 %collective-permute-done.21.refs_0_ = bf16[32,7296]{1,0:T(8,128)(2,1)S(1)} collective-permute-done((bf16[32,7296]{1,0:T(8,128)(2,1)S(1)}, bf16[32,7296]{1,0:T(8,128)(2,1)S(1)}, u32[]{:S(2)}, u32[]{:S(2)}) %collective-permute-start.21) | collective-permute-done | bytes 466976 | tf_op jit(solution)/shard_map/relay1/ppermute | solution.py:33
  149.9 5.8 %collective-permute-done.29.refs_2_ = bf16[32,7296]{1,0:T(8,128)(2,1)S(1)} collective-permute-done((bf16[32,7296]{1,0:T(8,128)(2,1)S(1)}, bf16[32,7296]{1,0:T(8,128)(2,1)S(1)}, u32[]{:S(2)}, u32[]{:S(2)}) %collective-permute-start.29) | collective-permute-done | bytes 466976 | tf_op jit(solution)/shard_map/relay0/ppermute | solution.py:33
  155.8 7.8 %collective-permute-done.30.refs_3_ = bf16[32,7296]{1,0:T(8,128)(2,1)S(1)} collective-permute-done((bf16[32,7296]{1,0:T(8,128)(2,1)S(1)}, bf16[32,7296]{1,0:T(8,128)(2,1)S(1)}, u32[]{:S(2)}, u32[]{:S(2)}) %collective-permute-start.30) | collective-permute-done | bytes 466976 | tf_op jit(solution)/shard_map/relay0/ppermute | solution.py:33
  (56 shorter events, 42.8 us)
Async XLA Ops:
  0.6 9.8 %collective-permute-start.3 = (bf16[7168,128]{1,0:T(8,128)(2,1)}, bf16[7168,128]{1,0:T(8,128)(2,1)S(1)}, u32[]{:S(2)}, u32[]{:S(2)}) collective-permute-start(bf16[7168,128]{1,0:T(8,128)(2,1)} %bitcast.14), channel_id=1, source_target_pairs={{0,1},{1,0},{2,3},{3,2},{4,5},{5,4},{6,7},{7,6},{8,9},{9,8},{10,11... | collective-permute-start | bytes 5505032 | tf_op jit(solution)/shard_map/weights/ppermute | solution.py:33
  4.9 23.3 %collective-permute-start.2 = (bf16[64,7296]{1,0:T(8,128)(2,1)}, bf16[64,7296]{1,0:T(8,128)(2,1)}, u32[]{:S(2)}, u32[]{:S(2)}) collective-permute-start(bf16[64,7296]{1,0:T(8,128)(2,1)} %get-tuple-element.48), channel_id=1, source_target_pairs={{0,8},{1,9},{2,10},{3,11},{4,12},{5,13},{6,14},{7,15},{8,0},{9,1},... | collective-permute-start | bytes 2801672 | tf_op jit(solution)/shard_map/swap/ppermute | solution.py:33
  6.9 13.6 %collective-permute-start = (bf16[32,7296]{1,0:T(8,128)(2,1)S(1)}, bf16[32,7296]{1,0:T(8,128)(2,1)S(1)}, u32[]{:S(2)}, u32[]{:S(2)}) collective-permute-start(bf16[32,7296]{1,0:T(8,128)(2,1)S(1)} %get-tuple-element.61.d.refs_0_), channel_id=1, source_target_pairs={{0,2},{1,3},{2,4},{3,5},{4,6},{5,7},{6,0},{7,1},{8,10},{9,11},{10,... | collective-permute-start | bytes 1400840 | tf_op jit(solution)/shard_map/first1/ppermute | solution.py:33
  8.4 13.7 %collective-permute-start.1 = (bf16[32,7296]{1,0:T(8,128)(2,1)S(1)}, bf16[32,7296]{1,0:T(8,128)(2,1)}, u32[]{:S(2)}, u32[]{:S(2)}) collective-permute-start(bf16[32,7296]{1,0:T(8,128)(2,1)S(1)} %get-tuple-element.62.b.refs_1_), channel_id=1, source_target_pairs={{0,6},{1,7},{2,0},{3,1},{4,2},{5,3},{6,4},{7,5},{8,14},{9,15},{10,... | collective-permute-start | bytes 1400840 | tf_op jit(solution)/shard_map/first1/ppermute | solution.py:33
  10.4 19.9 %collective-permute-start.5 = (bf16[128,1792]{1,0:T(8,128)(2,1)S(1)}, bf16[128,1792]{1,0:T(8,128)(2,1)S(1)}, u32[]{:S(2)}, u32[]{:S(2)}) collective-permute-start(bf16[128,1792]{1,0:T(8,128)(2,1)S(1)} %get-tuple-element.52), channel_id=1, source_target_pairs={{0,2},{1,3},{2,4},{3,5},{4,6},{5,7},{6,0},{7,1},{8,10},{9,11},{10,... | collective-permute-start | bytes 1376264 | tf_op jit(solution)/shard_map/down/ppermute | solution.py:33
  12.0 19.2 %collective-permute-start.6 = (bf16[128,1792]{1,0:T(8,128)(2,1)S(1)}, bf16[128,1792]{1,0:T(8,128)(2,1)S(1)}, u32[]{:S(2)}, u32[]{:S(2)}) collective-permute-start(bf16[128,1792]{1,0:T(8,128)(2,1)S(1)} %get-tuple-element.53), channel_id=1, source_target_pairs={{0,6},{1,7},{2,0},{3,1},{4,2},{5,3},{6,4},{7,5},{8,14},{9,15},{10,... | collective-permute-start | bytes 1376264 | tf_op jit(solution)/shard_map/down/ppermute | solution.py:33
  22.1 20.2 %collective-permute-start.9 = (bf16[128,1792]{1,0:T(8,128)(2,1)S(1)}, bf16[128,1792]{1,0:T(8,128)(2,1)S(1)}, u32[]{:S(2)}, u32[]{:S(2)}) collective-permute-start(bf16[128,1792]{1,0:T(8,128)(2,1)S(1)} %get-tuple-element.60), channel_id=1, source_target_pairs={{0,4},{1,5},{2,6},{3,7},{4,0},{5,1},{6,2},{7,3},{8,12},{9,13},{10,... | collective-permute-start | bytes 1376264 | tf_op jit(solution)/shard_map/down/ppermute | solution.py:33
  32.3 29.1 %collective-permute-start.7 = (bf16[64,7296]{1,0:T(8,128)(2,1)S(1)}, bf16[64,7296]{1,0:T(8,128)(2,1)S(1)}, u32[]{:S(2)}, u32[]{:S(2)}) collective-permute-start(bf16[64,7296]{1,0:T(8,128)(2,1)S(1)} %get-tuple-element.56), channel_id=1, source_target_pairs={{0,2},{1,3},{2,4},{3,5},{4,6},{5,7},{6,0},{7,1},{8,10},{9,11},{10,... | collective-permute-start | bytes 2801672 | tf_op jit(solution)/shard_map/second1/ppermute | solution.py:33
  34.2 30.6 %collective-permute-start.8 = (bf16[64,7296]{1,0:T(8,128)(2,1)S(1)}, bf16[64,7296]{1,0:T(8,128)(2,1)S(1)}, u32[]{:S(2)}, u32[]{:S(2)}) collective-permute-start(bf16[64,7296]{1,0:T(8,128)(2,1)S(1)} %get-tuple-element.57), channel_id=1, source_target_pairs={{0,6},{1,7},{2,0},{3,1},{4,2},{5,3},{6,4},{7,5},{8,14},{9,15},{10,... | collective-permute-start | bytes 2801672 | tf_op jit(solution)/shard_map/second1/ppermute | solution.py:33
  42.9 22.0 %collective-permute-start.10 = (bf16[512,1792]{1,0:T(8,128)(2,1)S(1)}, bf16[512,1792]{1,0:T(8,128)(2,1)S(1)}, u32[]{:S(2)}, u32[]{:S(2)}) collective-permute-start(bf16[512,1792]{1,0:T(8,128)(2,1)S(1)} %stack.13.refs_10_), channel_id=1, source_target_pairs={{0,1},{1,0},{2,3},{3,2},{4,5},{5,4},{6,7},{7,6},{8,9},{9,8},{10,11... | collective-permute-start | bytes 5505032 | tf_op jit(solution)/shard_map/down/ppermute | solution.py:33
  44.3 29.3 %collective-permute-start.17 = (bf16[32,7296]{1,0:T(8,128)(2,1)S(1)}, bf16[32,7296]{1,0:T(8,128)(2,1)S(1)}, u32[]{:S(2)}, u32[]{:S(2)}) collective-permute-start(bf16[32,7296]{1,0:T(8,128)(2,1)S(1)} %get-tuple-element.91.d.refs_0_), channel_id=1, source_target_pairs={{0,2},{1,3},{2,4},{3,5},{4,6},{5,7},{6,0},{7,1},{8,10},{9,11},{10,... | collective-permute-start | bytes 1400840 | tf_op jit(solution)/shard_map/first0/ppermute | solution.py:33
  45.4 28.3 %collective-permute-start.18 = (bf16[32,7296]{1,0:T(8,128)(2,1)S(1)}, bf16[32,7296]{1,0:T(8,128)(2,1)S(1)}, u32[]{:S(2)}, u32[]{:S(2)}) collective-permute-start(bf16[32,7296]{1,0:T(8,128)(2,1)S(1)} %get-tuple-element.90.b.refs_1_), channel_id=1, source_target_pairs={{0,6},{1,7},{2,0},{3,1},{4,2},{5,3},{6,4},{7,5},{8,14},{9,15},{10,... | collective-permute-start | bytes 1400840 | tf_op jit(solution)/shard_map/first0/ppermute | solution.py:33
  78.4 17.9 %collective-permute-start.19 = (bf16[64,7296]{1,0:T(8,128)(2,1)S(1)}, bf16[64,7296]{1,0:T(8,128)(2,1)S(1)}, u32[]{:S(2)}, u32[]{:S(2)}) collective-permute-start(bf16[64,7296]{1,0:T(8,128)(2,1)S(1)} %get-tuple-element.74), channel_id=1, source_target_pairs={{0,2},{1,3},{2,4},{3,5},{4,6},{5,7},{6,0},{7,1},{8,10},{9,11},{10,... | collective-permute-start | bytes 2801672 | tf_op jit(solution)/shard_map/second0/ppermute | solution.py:33
  80.6 21.1 %collective-permute-start.20 = (bf16[64,7296]{1,0:T(8,128)(2,1)S(1)}, bf16[64,7296]{1,0:T(8,128)(2,1)S(1)}, u32[]{:S(2)}, u32[]{:S(2)}) collective-permute-start(bf16[64,7296]{1,0:T(8,128)(2,1)S(1)} %get-tuple-element.75), channel_id=1, source_target_pairs={{0,6},{1,7},{2,0},{3,1},{4,2},{5,3},{6,4},{7,5},{8,14},{9,15},{10,... | collective-permute-start | bytes 2801672 | tf_op jit(solution)/shard_map/second0/ppermute | solution.py:33
  82.8 37.0 %collective-permute-start.14 = (bf16[64,1792]{1,0:T(8,128)(2,1)S(1)}, bf16[64,1792]{1,0:T(8,128)(2,1)S(1)}, u32[]{:S(2)}, u32[]{:S(2)}) collective-permute-start(bf16[64,1792]{1,0:T(8,128)(2,1)S(1)} %get-tuple-element.68), channel_id=1, source_target_pairs={{0,6},{1,7},{2,0},{3,1},{4,2},{5,3},{6,4},{7,5},{8,14},{9,15},{10,... | collective-permute-start | bytes 688136 | tf_op jit(solution)/shard_map/back1/ppermute | solution.py:33
  109.7 16.5 %collective-permute-start.15 = (bf16[64,1792]{1,0:T(8,128)(2,1)S(1)}, bf16[64,1792]{1,0:T(8,128)(2,1)S(1)}, u32[]{:S(2)}, u32[]{:S(2)}) collective-permute-start(bf16[64,1792]{1,0:T(8,128)(2,1)S(1)} %get-tuple-element.69), channel_id=1, source_target_pairs={{0,2},{1,3},{2,4},{3,5},{4,6},{5,7},{6,0},{7,1},{8,10},{9,11},{10,... | collective-permute-start | bytes 688136 | tf_op jit(solution)/shard_map/back1/ppermute | solution.py:33
  111.1 15.0 %collective-permute-start.16 = (bf16[64,1792]{1,0:T(8,128)(2,1)S(1)}, bf16[64,1792]{1,0:T(8,128)(2,1)S(1)}, u32[]{:S(2)}, u32[]{:S(2)}) collective-permute-start(bf16[64,1792]{1,0:T(8,128)(2,1)S(1)} %get-tuple-element.70), channel_id=1, source_target_pairs={{0,4},{1,5},{2,6},{3,7},{4,0},{5,1},{6,2},{7,3},{8,12},{9,13},{10,... | collective-permute-start | bytes 688136 | tf_op jit(solution)/shard_map/back1/ppermute | solution.py:33
  117.7 17.7 %collective-permute-start.26 = (bf16[64,1792]{1,0:T(8,128)(2,1)S(1)}, bf16[64,1792]{1,0:T(8,128)(2,1)S(1)}, u32[]{:S(2)}, u32[]{:S(2)}) collective-permute-start(bf16[64,1792]{1,0:T(8,128)(2,1)S(1)} %get-tuple-element.83), channel_id=1, source_target_pairs={{0,6},{1,7},{2,0},{3,1},{4,2},{5,3},{6,4},{7,5},{8,14},{9,15},{10,... | collective-permute-start | bytes 688136 | tf_op jit(solution)/shard_map/back0/ppermute | solution.py:33
  118.8 16.6 %collective-permute-start.27 = (bf16[64,1792]{1,0:T(8,128)(2,1)S(1)}, bf16[64,1792]{1,0:T(8,128)(2,1)S(1)}, u32[]{:S(2)}, u32[]{:S(2)}) collective-permute-start(bf16[64,1792]{1,0:T(8,128)(2,1)S(1)} %get-tuple-element.84), channel_id=1, source_target_pairs={{0,2},{1,3},{2,4},{3,5},{4,6},{5,7},{6,0},{7,1},{8,10},{9,11},{10,... | collective-permute-start | bytes 688136 | tf_op jit(solution)/shard_map/back0/ppermute | solution.py:33
  119.8 15.6 %collective-permute-start.28 = (bf16[64,1792]{1,0:T(8,128)(2,1)S(1)}, bf16[64,1792]{1,0:T(8,128)(2,1)S(1)}, u32[]{:S(2)}, u32[]{:S(2)}) collective-permute-start(bf16[64,1792]{1,0:T(8,128)(2,1)S(1)} %get-tuple-element.85), channel_id=1, source_target_pairs={{0,4},{1,5},{2,6},{3,7},{4,0},{5,1},{6,2},{7,3},{8,12},{9,13},{10,... | collective-permute-start | bytes 688136 | tf_op jit(solution)/shard_map/back0/ppermute | solution.py:33
  126.2 23.7 %collective-permute-start.21 = (bf16[32,7296]{1,0:T(8,128)(2,1)S(1)}, bf16[32,7296]{1,0:T(8,128)(2,1)S(1)}, u32[]{:S(2)}, u32[]{:S(2)}) collective-permute-start(bf16[32,7296]{1,0:T(8,128)(2,1)S(1)} %get-tuple-element.80), channel_id=1, source_target_pairs={{0,16},{1,17},{2,18},{3,19},{4,20},{5,21},{6,22},{7,23},{8,24},{9,... | collective-permute-start | bytes 1400840 | tf_op jit(solution)/shard_map/relay1/ppermute | solution.py:33
  131.4 18.5 %collective-permute-start.22 = (bf16[32,7296]{1,0:T(8,128)(2,1)S(1)}, bf16[32,7296]{1,0:T(8,128)(2,1)S(1)}, u32[]{:S(2)}, u32[]{:S(2)}) collective-permute-start(bf16[32,7296]{1,0:T(8,128)(2,1)S(1)} %get-tuple-element.81), channel_id=1, source_target_pairs={{16,0},{17,1},{18,2},{19,3},{20,4},{21,5},{22,6},{23,7},{24,8},{25... | collective-permute-start | bytes 1400840 | tf_op jit(solution)/shard_map/relay1/ppermute | solution.py:33
  136.2 19.6 %collective-permute-start.29 = (bf16[32,7296]{1,0:T(8,128)(2,1)S(1)}, bf16[32,7296]{1,0:T(8,128)(2,1)S(1)}, u32[]{:S(2)}, u32[]{:S(2)}) collective-permute-start(bf16[32,7296]{1,0:T(8,128)(2,1)S(1)} %get-tuple-element.86), channel_id=1, source_target_pairs={{0,24},{1,25},{2,26},{3,27},{4,28},{5,29},{6,30},{7,31},{8,16},{9,... | collective-permute-start | bytes 1400840 | tf_op jit(solution)/shard_map/relay0/ppermute | solution.py:33
  140.1 23.4 %collective-permute-start.30 = (bf16[32,7296]{1,0:T(8,128)(2,1)S(1)}, bf16[32,7296]{1,0:T(8,128)(2,1)S(1)}, u32[]{:S(2)}, u32[]{:S(2)}) collective-permute-start(bf16[32,7296]{1,0:T(8,128)(2,1)S(1)} %get-tuple-element.87), channel_id=1, source_target_pairs={{16,8},{17,9},{18,10},{19,11},{20,12},{21,13},{22,14},{23,15},{24,... | collective-permute-start | bytes 1400840 | tf_op jit(solution)/shard_map/relay0/ppermute | solution.py:33
  (9 other events, 95.2 us)

commit v3 on v2

--- a/solution.py
+++ b/solution.py
@@ -33,18 +33,6 @@
     return lax.ppermute(shard, ("pipe", "ep"), pairs)
 
 
-def picks(routes, expert, capacity):
-    count = routes.shape[1]
-    match = (routes == expert).astype(jnp.float32)
-    upto = (
-        lax.broadcasted_iota(jnp.int32, (count, count), 0)
-        <= lax.broadcasted_iota(jnp.int32, (count, count), 1)
-    ).astype(jnp.float32)
-    rank = jnp.dot(match, upto, preferred_element_type=jnp.float32)
-    slots = lax.broadcasted_iota(jnp.int32, (capacity, count), 0).astype(jnp.float32) + 1.0
-    return jnp.where((rank == slots) & (match > 0.0), 1.0, 0.0)
-
-
 def slices_kernel(x_ref, down, *refs):
     outs, sems = refs[:-1], refs[-1]
     columns = outs[0].shape[1]
@@ -90,39 +78,48 @@
         copy.start()
     mine, z = place[0], place[1]
     every = fr.shape[1]
-    lane = lax.broadcasted_iota(jnp.int32, (capacity, 128), 1)
-    token = lax.broadcasted_iota(jnp.int32, (capacity, count), 1).astype(jnp.float32)
+    lane = lax.broadcasted_iota(jnp.int32, (count, 128), 1)
+    token = lax.broadcasted_iota(jnp.int32, (count, count), 1).astype(jnp.float32)
     local = (
         lax.broadcasted_iota(jnp.int32, (every, count), 0)
         == lax.broadcasted_iota(jnp.int32, (every, count), 1) + mine * count
     ).astype(jnp.bfloat16)
     for copy in copies[:4]:
         copy.wait()
+    upto = (
+        lax.broadcasted_iota(jnp.int32, (count, count), 0)
+        <= lax.broadcasted_iota(jnp.int32, (count, count), 1)
+    ).astype(jnp.bfloat16)
+    row = lax.broadcasted_iota(jnp.int32, (count, count), 0)
+    wanted = jnp.where(row < capacity, z, 1 - z).astype(jnp.float32)
+    slot = (jnp.where(row < capacity, row, row - capacity) + 1).astype(jnp.float32)
     found = []
     for routes, share in ((fr_v, fs_v), (rr_v, rs_v)):
         routes = jnp.dot(
             routes[...].astype(jnp.bfloat16), local, preferred_element_type=jnp.float32
         )
-        routes = (routes > 0.5).astype(jnp.int32)
-        for expert in (z, 1 - z):
-            pick = picks(routes, expert, capacity)
-            rest = jnp.sum(pick * share[...], axis=1, keepdims=True)
-            tail = jnp.where(lane == 3, jnp.sum(pick * token, axis=1, keepdims=True), 0.0)
-            for at_term in range(3):
-                term = rest.astype(jnp.bfloat16).astype(jnp.float32)
-                tail = jnp.where(lane == at_term, term, tail)
-                rest = rest - term
-            found.append((pick.astype(jnp.bfloat16), tail.astype(jnp.bfloat16)))
+        match = jnp.broadcast_to(routes, (count, count)) == wanted
+        rank = jnp.dot(
+            jnp.where(match, 1.0, 0.0).astype(jnp.bfloat16),
+            upto,
+            preferred_element_type=jnp.float32,
+        )
+        pick = jnp.where(match & (rank == slot), 1.0, 0.0)
+        rest = jnp.sum(pick * share[...], axis=1, keepdims=True)
+        tail = jnp.where(lane == 3, jnp.sum(pick * token, axis=1, keepdims=True), 0.0)
+        for at_term in range(3):
+            term = rest.astype(jnp.bfloat16).astype(jnp.float32)
+            tail = jnp.where(lane == at_term, term, tail)
+            rest = rest - term
+        found.append((pick.astype(jnp.bfloat16), tail.astype(jnp.bfloat16)))
     for at, rows in enumerate((fx_v, rx_v)):
         copies[4 + at].wait()
-        for side in range(2):
-            pick, tail = found[2 * at + side]
-            out = oth if side else (own_f, own_r)[at]
-            part = slice(at * capacity, (at + 1) * capacity) if side else slice(None)
-            out[part, :width] = jnp.dot(
-                pick, rows[...], preferred_element_type=jnp.float32
-            ).astype(jnp.bfloat16)
-            out[part, width:] = tail
+        pick, tail = found[at]
+        own = (own_f, own_r)[at]
+        part = slice(at * capacity, (at + 1) * capacity)
+        both = jnp.dot(pick, rows[...], preferred_element_type=jnp.float32).astype(jnp.bfloat16)
+        own[:, :width], oth[part, :width] = both[:capacity], both[capacity:]
+        own[:, width:], oth[part, width:] = tail[:capacity], tail[capacity:]
 
 
 def pack(place, *arrays):
@@ -421,7 +418,7 @@
         return [f, r, left_f, right_r, onward, backward]
 
     with jax.named_scope("second1"):
-        rows1 = gather(own_f, own_r, own_left_f, own_right_r, [swapped] + parts[1:3])
+        rows1 = gather(own_f, own_r, own_left_f, own_right_r, parts[1:3])
     with jax.named_scope("down"):
         half_down = stack(parts)
         down = [half_down, send(half_down, core=True)]

time: 166 us -> 166 us (level)
  no operation moved by 1% of the time
where the time goes in v3:
time: 166 us
  waiting for transfers between devices  80.9 us (49%)
  starting transfers between devices  62.3 us (38%)
  Pallas kernels  20.2 us (12%)
    ppermute x31, waiting for transfers between devices, move(): return lax.ppermute(shard, ('pipe', 'ep'), pairs)  80.9 us
    ppermute x31, starting transfers between devices, move(): return lax.ppermute(shard, ('pipe', 'ep'), pairs)  62.3 us
    pallas_call x2, Pallas kernels, hidden_rows(): pl.pallas_call(functools.partial(hidden_kernel, 7, plan), in_specs=[whole...  7.32 us
    pallas_call x1, Pallas kernels, pack(): pl.pallas_call(pack_kernel, in_specs=[pl.BlockSpec(memory_space=pltpu.SME...  3.57 us
    pallas_call x2, Pallas kernels, out_rows(): pl.pallas_call(functools.partial(out_kernel, 7, plan), in_specs=[pl.Block...  3.35 us
  transfers between devices with their start and end apart: 31, of which 19 were waited for; matrix products, arithmetic and copies ran while one was open for 1% of the time, Pallas kernels for 11%

profile of v3, /device:TPU:10, one launch (start us, length us, event | category | flops | bytes accessed | tf_op | source)
XLA Modules:
  0.0 165.6 jit_solution(12310982916128186937)
XLA Ops:
  1.3 3.6 %pack.1 = (bf16[32,7296]{1,0:T(8,128)(2,1)S(1)}, bf16[32,7296]{1,0:T(8,128)(2,1)S(1)}, bf16[64,7296]{1,0:T(8,128)(2,1)}) custom-call(s32[2]{0:T(128)S(1)} %pad_add_fusion.place, s32[1,1024]{1,0:T(1,128)} %bitcast.23, s32[1,1024]{1,0:T(1,128)} %bitcast.24, f32[1,64]{1,0:T(1,128)} %bitcast.25, f32[1,64]{1,0:T(1,128)} %bitcast.26, bf16[64,7168]{1,0:T(8,128)(2,1)} %bitcast.21, ...), custom_call_target="tpu_custom_call" | custom-call | tf_op jit(solution)/shard_map/pack/pack/pallas_call | solution.py:128
  12.5 8.0 %collective-permute-done.a.refs_2_ = bf16[32,7296]{1,0:T(8,128)(2,1)S(1)} collective-permute-done((bf16[32,7296]{1,0:T(8,128)(2,1)S(1)}, bf16[32,7296]{1,0:T(8,128)(2,1)S(1)}, u32[]{:S(2)}, u32[]{:S(2)}) %collective-permute-start) | collective-permute-done | bytes 466976 | tf_op jit(solution)/shard_map/first1/ppermute | solution.py:33
  24.4 5.9 %collective-permute-done.4.refs_1_ = bf16[128,1792]{1,0:T(8,128)(2,1)S(1)} collective-permute-done((bf16[128,1792]{1,0:T(8,128)(2,1)S(1)}, bf16[128,1792]{1,0:T(8,128)(2,1)S(1)}, u32[]{:S(2)}, u32[]{:S(2)}) %collective-permute-start.4) | collective-permute-done | bytes 458784 | tf_op jit(solution)/shard_map/down/ppermute | solution.py:33
  34.3 5.6 %collective-permute-start.7 = (bf16[64,7296]{1,0:T(8,128)(2,1)S(1)}, bf16[64,7296]{1,0:T(8,128)(2,1)S(1)}, u32[]{:S(2)}, u32[]{:S(2)}) collective-permute-start(bf16[64,7296]{1,0:T(8,128)(2,1)S(1)} %get-tuple-element.56), channel_id=1, source_target_pairs={{0,6},{1,7},{2,0},{3,1},{4,2},{5,3},{6,4},{7,5},{8,14},{9,15},{10,... | collective-permute-start | bytes 2801672 | tf_op jit(solution)/shard_map/second1/ppermute | solution.py:33
  39.8 2.5 %collective-permute-done.8.refs_3_ = bf16[128,1792]{1,0:T(8,128)(2,1)S(1)} collective-permute-done((bf16[128,1792]{1,0:T(8,128)(2,1)S(1)}, bf16[128,1792]{1,0:T(8,128)(2,1)S(1)}, u32[]{:S(2)}, u32[]{:S(2)}) %collective-permute-start.8) | collective-permute-done | bytes 458784 | tf_op jit(solution)/shard_map/down/ppermute | solution.py:33
  46.4 14.9 %collective-permute-done.6.refs_4_ = bf16[64,7296]{1,0:T(8,128)(2,1)S(1)} collective-permute-done((bf16[64,7296]{1,0:T(8,128)(2,1)S(1)}, bf16[64,7296]{1,0:T(8,128)(2,1)S(1)}, u32[]{:S(2)}, u32[]{:S(2)}) %collective-permute-start.6) | collective-permute-done | bytes 933920 | tf_op jit(solution)/shard_map/second1/ppermute | solution.py:33
  61.4 3.5 %collective-permute-done.7.refs_5_ = bf16[64,7296]{1,0:T(8,128)(2,1)S(1)} collective-permute-done((bf16[64,7296]{1,0:T(8,128)(2,1)S(1)}, bf16[64,7296]{1,0:T(8,128)(2,1)S(1)}, u32[]{:S(2)}, u32[]{:S(2)}) %collective-permute-start.7) | collective-permute-done | bytes 933920 | tf_op jit(solution)/shard_map/second1/ppermute | solution.py:33
  64.9 3.7 %hidden.2.refs_6_ = bf16[256,256]{1,0:T(8,128)(2,1)S(1)} custom-call(bf16[32,7296]{1,0:T(8,128)(2,1)S(1)} %get-tuple-element.60.d.refs_0_, bf16[32,7296]{1,0:T(8,128)(2,1)S(1)} %get-tuple-element.61.b.refs_1_, bf16[32,7296]{1,0:T(8,128)(2,1)S(1)} %collective-permute-done.a.refs_2_, bf16[32,7296]{1,0:T(8,128)(2,1)} %collective-permute-done.1.c.refs_3_, ...), custom_call_target="tpu_custom_call" | custom-call | flops 1879048192 | bytes 11010048 | tf_op jit(solution)/shard_map/hidden1/hidden/pallas_call | solution.py:173
  70.9 2.6 %collective-permute-start.12 = (bf16[256,256]{1,0:T(8,128)(2,1)S(1)}, bf16[256,256]{1,0:T(8,128)(2,1)S(1)}, u32[]{:S(2)}, u32[]{:S(2)}) collective-permute-start(bf16[256,256]{1,0:T(8,128)(2,1)S(1)} %hidden.2.refs_6_), channel_id=1, source_target_pairs={{0,4},{1,5},{2,6},{3,7},{4,0},{5,1},{6,2},{7,3},{8,12},{9,13},{10,... | collective-permute-start | bytes 393224 | tf_op jit(solution)/shard_map/hidden1/ppermute | solution.py:33
  75.4 2.9 %collective-permute-done.12.refs_9_ = bf16[256,256]{1,0:T(8,128)(2,1)S(1)} collective-permute-done((bf16[256,256]{1,0:T(8,128)(2,1)S(1)}, bf16[256,256]{1,0:T(8,128)(2,1)S(1)}, u32[]{:S(2)}, u32[]{:S(2)}) %collective-permute-start.12) | collective-permute-done | bytes 131104 | tf_op jit(solution)/shard_map/hidden1/ppermute | solution.py:33
  82.8 3.1 %collective-permute-start.13 = (bf16[64,1792]{1,0:T(8,128)(2,1)S(1)}, bf16[64,1792]{1,0:T(8,128)(2,1)S(1)}, u32[]{:S(2)}, u32[]{:S(2)}) collective-permute-start(bf16[64,1792]{1,0:T(8,128)(2,1)S(1)} %get-tuple-element.67), channel_id=1, source_target_pairs={{0,6},{1,7},{2,0},{3,1},{4,2},{5,3},{6,4},{7,5},{8,14},{9,15},{10,... | collective-permute-start | bytes 688136 | tf_op jit(solution)/shard_map/back1/ppermute | solution.py:33
  85.9 10.5 %collective-permute-done.19.refs_4_ = bf16[64,7296]{1,0:T(8,128)(2,1)S(1)} collective-permute-done((bf16[64,7296]{1,0:T(8,128)(2,1)S(1)}, bf16[64,7296]{1,0:T(8,128)(2,1)S(1)}, u32[]{:S(2)}, u32[]{:S(2)}) %collective-permute-start.19) | collective-permute-done | bytes 933920 | tf_op jit(solution)/shard_map/second0/ppermute | solution.py:33
  96.4 5.3 %collective-permute-done.20.refs_5_ = bf16[64,7296]{1,0:T(8,128)(2,1)S(1)} collective-permute-done((bf16[64,7296]{1,0:T(8,128)(2,1)S(1)}, bf16[64,7296]{1,0:T(8,128)(2,1)S(1)}, u32[]{:S(2)}, u32[]{:S(2)}) %collective-permute-start.20) | collective-permute-done | bytes 933920 | tf_op jit(solution)/shard_map/second0/ppermute | solution.py:33
  101.6 3.6 %hidden.3.refs_6_ = bf16[256,256]{1,0:T(8,128)(2,1)S(1)} custom-call(bf16[32,7296]{1,0:T(8,128)(2,1)S(1)} %get-tuple-element.91.d.refs_0_, bf16[32,7296]{1,0:T(8,128)(2,1)S(1)} %get-tuple-element.90.b.refs_1_, bf16[32,7296]{1,0:T(8,128)(2,1)S(1)} %collective-permute-done.17.a.refs_2_, bf16[32,7296]{1,0:T(8,128)(2,1)S(1)} %collective-permute-done.18.c.refs_3_, ...), custom_call_target="tpu_custom_call" | custom-call | flops 1879048192 | bytes 11010048 | tf_op jit(solution)/shard_map/hidden0/hidden/pallas_call | solution.py:173
  111.1 2.8 %collective-permute-start.15 = (bf16[64,1792]{1,0:T(8,128)(2,1)S(1)}, bf16[64,1792]{1,0:T(8,128)(2,1)S(1)}, u32[]{:S(2)}, u32[]{:S(2)}) collective-permute-start(bf16[64,1792]{1,0:T(8,128)(2,1)S(1)} %get-tuple-element.69), channel_id=1, source_target_pairs={{0,4},{1,5},{2,6},{3,7},{4,0},{5,1},{6,2},{7,3},{8,12},{9,13},{10,... | collective-permute-start | bytes 688136 | tf_op jit(solution)/shard_map/back1/ppermute | solution.py:33
  114.0 2.5 %collective-permute-done.25.refs_9_ = bf16[256,256]{1,0:T(8,128)(2,1)S(1)} collective-permute-done((bf16[256,256]{1,0:T(8,128)(2,1)S(1)}, bf16[256,256]{1,0:T(8,128)(2,1)S(1)}, u32[]{:S(2)}, u32[]{:S(2)}) %collective-permute-start.25) | collective-permute-done | bytes 131104 | tf_op jit(solution)/shard_map/hidden0/ppermute | solution.py:33
  119.7 6.4 %collective-permute-start.28 = (bf16[64,1792]{1,0:T(8,128)(2,1)S(1)}, bf16[64,1792]{1,0:T(8,128)(2,1)S(1)}, u32[]{:S(2)}, u32[]{:S(2)}) collective-permute-start(bf16[64,1792]{1,0:T(8,128)(2,1)S(1)} %get-tuple-element.85), channel_id=1, source_target_pairs={{0,4},{1,5},{2,6},{3,7},{4,0},{5,1},{6,2},{7,3},{8,12},{9,13},{10,... | collective-permute-start | bytes 688136 | tf_op jit(solution)/shard_map/back0/ppermute | solution.py:33
  126.2 5.1 %collective-permute-start.21 = (bf16[32,7296]{1,0:T(8,128)(2,1)S(1)}, bf16[32,7296]{1,0:T(8,128)(2,1)S(1)}, u32[]{:S(2)}, u32[]{:S(2)}) collective-permute-start(bf16[32,7296]{1,0:T(8,128)(2,1)S(1)} %get-tuple-element.80), channel_id=1, source_target_pairs={{0,16},{1,17},{2,18},{3,19},{4,20},{5,21},{6,22},{7,23},{8,24},{9,... | collective-permute-start | bytes 1400840 | tf_op jit(solution)/shard_map/relay1/ppermute | solution.py:33
  131.3 4.0 %collective-permute-start.22 = (bf16[32,7296]{1,0:T(8,128)(2,1)S(1)}, bf16[32,7296]{1,0:T(8,128)(2,1)S(1)}, u32[]{:S(2)}, u32[]{:S(2)}) collective-permute-start(bf16[32,7296]{1,0:T(8,128)(2,1)S(1)} %get-tuple-element.81), channel_id=1, source_target_pairs={{16,0},{17,1},{18,2},{19,3},{20,4},{21,5},{22,6},{23,7},{24,8},{25... | collective-permute-start | bytes 1400840 | tf_op jit(solution)/shard_map/relay1/ppermute | solution.py:33
  136.1 3.9 %collective-permute-start.29 = (bf16[32,7296]{1,0:T(8,128)(2,1)S(1)}, bf16[32,7296]{1,0:T(8,128)(2,1)S(1)}, u32[]{:S(2)}, u32[]{:S(2)}) collective-permute-start(bf16[32,7296]{1,0:T(8,128)(2,1)S(1)} %get-tuple-element.86), channel_id=1, source_target_pairs={{0,24},{1,25},{2,26},{3,27},{4,28},{5,29},{6,30},{7,31},{8,16},{9,... | collective-permute-start | bytes 1400840 | tf_op jit(solution)/shard_map/relay0/ppermute | solution.py:33
  140.0 4.0 %collective-permute-start.30 = (bf16[32,7296]{1,0:T(8,128)(2,1)S(1)}, bf16[32,7296]{1,0:T(8,128)(2,1)S(1)}, u32[]{:S(2)}, u32[]{:S(2)}) collective-permute-start(bf16[32,7296]{1,0:T(8,128)(2,1)S(1)} %get-tuple-element.87), channel_id=1, source_target_pairs={{16,8},{17,9},{18,10},{19,11},{20,12},{21,13},{22,14},{23,15},{24,... | collective-permute-start | bytes 1400840 | tf_op jit(solution)/shard_map/relay0/ppermute | solution.py:33
  144.0 5.1 %collective-permute-done.21.refs_0_ = bf16[32,7296]{1,0:T(8,128)(2,1)S(1)} collective-permute-done((bf16[32,7296]{1,0:T(8,128)(2,1)S(1)}, bf16[32,7296]{1,0:T(8,128)(2,1)S(1)}, u32[]{:S(2)}, u32[]{:S(2)}) %collective-permute-start.21) | collective-permute-done | bytes 466976 | tf_op jit(solution)/shard_map/relay1/ppermute | solution.py:33
  149.3 6.4 %collective-permute-done.29.refs_2_ = bf16[32,7296]{1,0:T(8,128)(2,1)S(1)} collective-permute-done((bf16[32,7296]{1,0:T(8,128)(2,1)S(1)}, bf16[32,7296]{1,0:T(8,128)(2,1)S(1)}, u32[]{:S(2)}, u32[]{:S(2)}) %collective-permute-start.29) | collective-permute-done | bytes 466976 | tf_op jit(solution)/shard_map/relay0/ppermute | solution.py:33
  155.7 8.0 %collective-permute-done.30.refs_3_ = bf16[32,7296]{1,0:T(8,128)(2,1)S(1)} collective-permute-done((bf16[32,7296]{1,0:T(8,128)(2,1)S(1)}, bf16[32,7296]{1,0:T(8,128)(2,1)S(1)}, u32[]{:S(2)}, u32[]{:S(2)}) %collective-permute-start.30) | collective-permute-done | bytes 466976 | tf_op jit(solution)/shard_map/relay0/ppermute | solution.py:33
  (56 shorter events, 40.9 us)
Async XLA Ops:
  0.6 9.7 %collective-permute-start.2 = (bf16[7168,128]{1,0:T(8,128)(2,1)}, bf16[7168,128]{1,0:T(8,128)(2,1)S(1)}, u32[]{:S(2)}, u32[]{:S(2)}) collective-permute-start(bf16[7168,128]{1,0:T(8,128)(2,1)} %bitcast.14), channel_id=1, source_target_pairs={{0,1},{1,0},{2,3},{3,2},{4,5},{5,4},{6,7},{7,6},{8,9},{9,8},{10,11... | collective-permute-start | bytes 5505032 | tf_op jit(solution)/shard_map/weights/ppermute | solution.py:33
  4.9 38.1 %collective-permute-start.16 = (bf16[64,7296]{1,0:T(8,128)(2,1)}, bf16[64,7296]{1,0:T(8,128)(2,1)}, u32[]{:S(2)}, u32[]{:S(2)}) collective-permute-start(bf16[64,7296]{1,0:T(8,128)(2,1)} %get-tuple-element.70), channel_id=1, source_target_pairs={{0,8},{1,9},{2,10},{3,11},{4,12},{5,13},{6,14},{7,15},{8,0},{9,1},... | collective-permute-start | bytes 2801672 | tf_op jit(solution)/shard_map/swap/ppermute | solution.py:33
  6.9 13.6 %collective-permute-start = (bf16[32,7296]{1,0:T(8,128)(2,1)S(1)}, bf16[32,7296]{1,0:T(8,128)(2,1)S(1)}, u32[]{:S(2)}, u32[]{:S(2)}) collective-permute-start(bf16[32,7296]{1,0:T(8,128)(2,1)S(1)} %get-tuple-element.60.d.refs_0_), channel_id=1, source_target_pairs={{0,2},{1,3},{2,4},{3,5},{4,6},{5,7},{6,0},{7,1},{8,10},{9,11},{10,... | collective-permute-start | bytes 1400840 | tf_op jit(solution)/shard_map/first1/ppermute | solution.py:33
  8.4 13.7 %collective-permute-start.1 = (bf16[32,7296]{1,0:T(8,128)(2,1)S(1)}, bf16[32,7296]{1,0:T(8,128)(2,1)}, u32[]{:S(2)}, u32[]{:S(2)}) collective-permute-start(bf16[32,7296]{1,0:T(8,128)(2,1)S(1)} %get-tuple-element.61.b.refs_1_), channel_id=1, source_target_pairs={{0,6},{1,7},{2,0},{3,1},{4,2},{5,3},{6,4},{7,5},{8,14},{9,15},{10,... | collective-permute-start | bytes 1400840 | tf_op jit(solution)/shard_map/first1/ppermute | solution.py:33
  10.4 19.9 %collective-permute-start.4 = (bf16[128,1792]{1,0:T(8,128)(2,1)S(1)}, bf16[128,1792]{1,0:T(8,128)(2,1)S(1)}, u32[]{:S(2)}, u32[]{:S(2)}) collective-permute-start(bf16[128,1792]{1,0:T(8,128)(2,1)S(1)} %get-tuple-element.51), channel_id=1, source_target_pairs={{0,2},{1,3},{2,4},{3,5},{4,6},{5,7},{6,0},{7,1},{8,10},{9,11},{10,... | collective-permute-start | bytes 1376264 | tf_op jit(solution)/shard_map/down/ppermute | solution.py:33
  12.0 19.2 %collective-permute-start.5 = (bf16[128,1792]{1,0:T(8,128)(2,1)S(1)}, bf16[128,1792]{1,0:T(8,128)(2,1)S(1)}, u32[]{:S(2)}, u32[]{:S(2)}) collective-permute-start(bf16[128,1792]{1,0:T(8,128)(2,1)S(1)} %get-tuple-element.52), channel_id=1, source_target_pairs={{0,6},{1,7},{2,0},{3,1},{4,2},{5,3},{6,4},{7,5},{8,14},{9,15},{10,... | collective-permute-start | bytes 1376264 | tf_op jit(solution)/shard_map/down/ppermute | solution.py:33
  22.1 20.2 %collective-permute-start.8 = (bf16[128,1792]{1,0:T(8,128)(2,1)S(1)}, bf16[128,1792]{1,0:T(8,128)(2,1)S(1)}, u32[]{:S(2)}, u32[]{:S(2)}) collective-permute-start(bf16[128,1792]{1,0:T(8,128)(2,1)S(1)} %get-tuple-element.59), channel_id=1, source_target_pairs={{0,4},{1,5},{2,6},{3,7},{4,0},{5,1},{6,2},{7,3},{8,12},{9,13},{10,... | collective-permute-start | bytes 1376264 | tf_op jit(solution)/shard_map/down/ppermute | solution.py:33
  32.3 29.0 %collective-permute-start.6 = (bf16[64,7296]{1,0:T(8,128)(2,1)S(1)}, bf16[64,7296]{1,0:T(8,128)(2,1)S(1)}, u32[]{:S(2)}, u32[]{:S(2)}) collective-permute-start(bf16[64,7296]{1,0:T(8,128)(2,1)S(1)} %get-tuple-element.55), channel_id=1, source_target_pairs={{0,2},{1,3},{2,4},{3,5},{4,6},{5,7},{6,0},{7,1},{8,10},{9,11},{10,... | collective-permute-start | bytes 2801672 | tf_op jit(solution)/shard_map/second1/ppermute | solution.py:33
  34.3 30.6 %collective-permute-start.7 = (bf16[64,7296]{1,0:T(8,128)(2,1)S(1)}, bf16[64,7296]{1,0:T(8,128)(2,1)S(1)}, u32[]{:S(2)}, u32[]{:S(2)}) collective-permute-start(bf16[64,7296]{1,0:T(8,128)(2,1)S(1)} %get-tuple-element.56), channel_id=1, source_target_pairs={{0,6},{1,7},{2,0},{3,1},{4,2},{5,3},{6,4},{7,5},{8,14},{9,15},{10,... | collective-permute-start | bytes 2801672 | tf_op jit(solution)/shard_map/second1/ppermute | solution.py:33
  42.9 22.0 %collective-permute-start.9 = (bf16[512,1792]{1,0:T(8,128)(2,1)S(1)}, bf16[512,1792]{1,0:T(8,128)(2,1)S(1)}, u32[]{:S(2)}, u32[]{:S(2)}) collective-permute-start(bf16[512,1792]{1,0:T(8,128)(2,1)S(1)} %stack.13.refs_10_), channel_id=1, source_target_pairs={{0,1},{1,0},{2,3},{3,2},{4,5},{5,4},{6,7},{7,6},{8,9},{9,8},{10,11... | collective-permute-start | bytes 5505032 | tf_op jit(solution)/shard_map/down/ppermute | solution.py:33
  44.3 29.2 %collective-permute-start.17 = (bf16[32,7296]{1,0:T(8,128)(2,1)S(1)}, bf16[32,7296]{1,0:T(8,128)(2,1)S(1)}, u32[]{:S(2)}, u32[]{:S(2)}) collective-permute-start(bf16[32,7296]{1,0:T(8,128)(2,1)S(1)} %get-tuple-element.91.d.refs_0_), channel_id=1, source_target_pairs={{0,2},{1,3},{2,4},{3,5},{4,6},{5,7},{6,0},{7,1},{8,10},{9,11},{10,... | collective-permute-start | bytes 1400840 | tf_op jit(solution)/shard_map/first0/ppermute | solution.py:33
  45.4 28.3 %collective-permute-start.18 = (bf16[32,7296]{1,0:T(8,128)(2,1)S(1)}, bf16[32,7296]{1,0:T(8,128)(2,1)S(1)}, u32[]{:S(2)}, u32[]{:S(2)}) collective-permute-start(bf16[32,7296]{1,0:T(8,128)(2,1)S(1)} %get-tuple-element.90.b.refs_1_), channel_id=1, source_target_pairs={{0,6},{1,7},{2,0},{3,1},{4,2},{5,3},{6,4},{7,5},{8,14},{9,15},{10,... | collective-permute-start | bytes 1400840 | tf_op jit(solution)/shard_map/first0/ppermute | solution.py:33
  78.4 17.9 %collective-permute-start.19 = (bf16[64,7296]{1,0:T(8,128)(2,1)S(1)}, bf16[64,7296]{1,0:T(8,128)(2,1)S(1)}, u32[]{:S(2)}, u32[]{:S(2)}) collective-permute-start(bf16[64,7296]{1,0:T(8,128)(2,1)S(1)} %get-tuple-element.74), channel_id=1, source_target_pairs={{0,2},{1,3},{2,4},{3,5},{4,6},{5,7},{6,0},{7,1},{8,10},{9,11},{10,... | collective-permute-start | bytes 2801672 | tf_op jit(solution)/shard_map/second0/ppermute | solution.py:33
  80.6 21.1 %collective-permute-start.20 = (bf16[64,7296]{1,0:T(8,128)(2,1)S(1)}, bf16[64,7296]{1,0:T(8,128)(2,1)S(1)}, u32[]{:S(2)}, u32[]{:S(2)}) collective-permute-start(bf16[64,7296]{1,0:T(8,128)(2,1)S(1)} %get-tuple-element.75), channel_id=1, source_target_pairs={{0,6},{1,7},{2,0},{3,1},{4,2},{5,3},{6,4},{7,5},{8,14},{9,15},{10,... | collective-permute-start | bytes 2801672 | tf_op jit(solution)/shard_map/second0/ppermute | solution.py:33
  82.8 37.0 %collective-permute-start.13 = (bf16[64,1792]{1,0:T(8,128)(2,1)S(1)}, bf16[64,1792]{1,0:T(8,128)(2,1)S(1)}, u32[]{:S(2)}, u32[]{:S(2)}) collective-permute-start(bf16[64,1792]{1,0:T(8,128)(2,1)S(1)} %get-tuple-element.67), channel_id=1, source_target_pairs={{0,6},{1,7},{2,0},{3,1},{4,2},{5,3},{6,4},{7,5},{8,14},{9,15},{10,... | collective-permute-start | bytes 688136 | tf_op jit(solution)/shard_map/back1/ppermute | solution.py:33
  109.6 16.5 %collective-permute-start.14 = (bf16[64,1792]{1,0:T(8,128)(2,1)S(1)}, bf16[64,1792]{1,0:T(8,128)(2,1)S(1)}, u32[]{:S(2)}, u32[]{:S(2)}) collective-permute-start(bf16[64,1792]{1,0:T(8,128)(2,1)S(1)} %get-tuple-element.68), channel_id=1, source_target_pairs={{0,2},{1,3},{2,4},{3,5},{4,6},{5,7},{6,0},{7,1},{8,10},{9,11},{10,... | collective-permute-start | bytes 688136 | tf_op jit(solution)/shard_map/back1/ppermute | solution.py:33
  111.1 15.0 %collective-permute-start.15 = (bf16[64,1792]{1,0:T(8,128)(2,1)S(1)}, bf16[64,1792]{1,0:T(8,128)(2,1)S(1)}, u32[]{:S(2)}, u32[]{:S(2)}) collective-permute-start(bf16[64,1792]{1,0:T(8,128)(2,1)S(1)} %get-tuple-element.69), channel_id=1, source_target_pairs={{0,4},{1,5},{2,6},{3,7},{4,0},{5,1},{6,2},{7,3},{8,12},{9,13},{10,... | collective-permute-start | bytes 688136 | tf_op jit(solution)/shard_map/back1/ppermute | solution.py:33
  117.6 17.6 %collective-permute-start.26 = (bf16[64,1792]{1,0:T(8,128)(2,1)S(1)}, bf16[64,1792]{1,0:T(8,128)(2,1)S(1)}, u32[]{:S(2)}, u32[]{:S(2)}) collective-permute-start(bf16[64,1792]{1,0:T(8,128)(2,1)S(1)} %get-tuple-element.83), channel_id=1, source_target_pairs={{0,6},{1,7},{2,0},{3,1},{4,2},{5,3},{6,4},{7,5},{8,14},{9,15},{10,... | collective-permute-start | bytes 688136 | tf_op jit(solution)/shard_map/back0/ppermute | solution.py:33
  118.7 16.5 %collective-permute-start.27 = (bf16[64,1792]{1,0:T(8,128)(2,1)S(1)}, bf16[64,1792]{1,0:T(8,128)(2,1)S(1)}, u32[]{:S(2)}, u32[]{:S(2)}) collective-permute-start(bf16[64,1792]{1,0:T(8,128)(2,1)S(1)} %get-tuple-element.84), channel_id=1, source_target_pairs={{0,2},{1,3},{2,4},{3,5},{4,6},{5,7},{6,0},{7,1},{8,10},{9,11},{10,... | collective-permute-start | bytes 688136 | tf_op jit(solution)/shard_map/back0/ppermute | solution.py:33
  119.7 15.5 %collective-permute-start.28 = (bf16[64,1792]{1,0:T(8,128)(2,1)S(1)}, bf16[64,1792]{1,0:T(8,128)(2,1)S(1)}, u32[]{:S(2)}, u32[]{:S(2)}) collective-permute-start(bf16[64,1792]{1,0:T(8,128)(2,1)S(1)} %get-tuple-element.85), channel_id=1, source_target_pairs={{0,4},{1,5},{2,6},{3,7},{4,0},{5,1},{6,2},{7,3},{8,12},{9,13},{10,... | collective-permute-start | bytes 688136 | tf_op jit(solution)/shard_map/back0/ppermute | solution.py:33
  126.2 23.0 %collective-permute-start.21 = (bf16[32,7296]{1,0:T(8,128)(2,1)S(1)}, bf16[32,7296]{1,0:T(8,128)(2,1)S(1)}, u32[]{:S(2)}, u32[]{:S(2)}) collective-permute-start(bf16[32,7296]{1,0:T(8,128)(2,1)S(1)} %get-tuple-element.80), channel_id=1, source_target_pairs={{0,16},{1,17},{2,18},{3,19},{4,20},{5,21},{6,22},{7,23},{8,24},{9,... | collective-permute-start | bytes 1400840 | tf_op jit(solution)/shard_map/relay1/ppermute | solution.py:33
  131.3 18.1 %collective-permute-start.22 = (bf16[32,7296]{1,0:T(8,128)(2,1)S(1)}, bf16[32,7296]{1,0:T(8,128)(2,1)S(1)}, u32[]{:S(2)}, u32[]{:S(2)}) collective-permute-start(bf16[32,7296]{1,0:T(8,128)(2,1)S(1)} %get-tuple-element.81), channel_id=1, source_target_pairs={{16,0},{17,1},{18,2},{19,3},{20,4},{21,5},{22,6},{23,7},{24,8},{25... | collective-permute-start | bytes 1400840 | tf_op jit(solution)/shard_map/relay1/ppermute | solution.py:33
  136.1 19.7 %collective-permute-start.29 = (bf16[32,7296]{1,0:T(8,128)(2,1)S(1)}, bf16[32,7296]{1,0:T(8,128)(2,1)S(1)}, u32[]{:S(2)}, u32[]{:S(2)}) collective-permute-start(bf16[32,7296]{1,0:T(8,128)(2,1)S(1)} %get-tuple-element.86), channel_id=1, source_target_pairs={{0,24},{1,25},{2,26},{3,27},{4,28},{5,29},{6,30},{7,31},{8,16},{9,... | collective-permute-start | bytes 1400840 | tf_op jit(solution)/shard_map/relay0/ppermute | solution.py:33
  140.0 23.8 %collective-permute-start.30 = (bf16[32,7296]{1,0:T(8,128)(2,1)S(1)}, bf16[32,7296]{1,0:T(8,128)(2,1)S(1)}, u32[]{:S(2)}, u32[]{:S(2)}) collective-permute-start(bf16[32,7296]{1,0:T(8,128)(2,1)S(1)} %get-tuple-element.87), channel_id=1, source_target_pairs={{16,8},{17,9},{18,10},{19,11},{20,12},{21,13},{22,14},{23,15},{24,... | collective-permute-start | bytes 1400840 | tf_op jit(solution)/shard_map/relay0/ppermute | solution.py:33
  (9 other events, 95.1 us)

commit v4 on v3

--- a/solution.py
+++ b/solution.py
@@ -437,7 +437,7 @@
     with jax.named_scope("hidden0"):
         hidden0 = spread(hidden_rows(rows0, plan, weights))
     with jax.named_scope("relay1"):
-        whole_f, whole_r = regroup(at_x, [own_f, own_r], after(back1, hidden0[:1]))
+        whole_f, whole_r = regroup(at_x, [own_f, own_r], after(back1, hidden0[1:]))
         sent1 = [send(whole_f, by=1), send(whole_r, by=-1)]
     with jax.named_scope("out0"):
         outs0 = out_rows(at_x, rows0, plan, hidden0, down)

time: 166 us -> 166 us (level)
  no operation moved by 1% of the time
where the time goes in v4:
time: 166 us
  waiting for transfers between devices  80.9 us (49%)
  starting transfers between devices  62.3 us (38%)
  Pallas kernels  20.2 us (12%)
    ppermute x31, waiting for transfers between devices, move(): return lax.ppermute(shard, ('pipe', 'ep'), pairs)  80.9 us
    ppermute x31, starting transfers between devices, move(): return lax.ppermute(shard, ('pipe', 'ep'), pairs)  62.3 us
    pallas_call x2, Pallas kernels, hidden_rows(): pl.pallas_call(functools.partial(hidden_kernel, 7, plan), in_specs=[whole...  7.32 us
    pallas_call x1, Pallas kernels, pack(): pl.pallas_call(pack_kernel, in_specs=[pl.BlockSpec(memory_space=pltpu.SME...  3.57 us
    pallas_call x2, Pallas kernels, out_rows(): pl.pallas_call(functools.partial(out_kernel, 7, plan), in_specs=[pl.Block...  3.35 us
  transfers between devices with their start and end apart: 31, of which 19 were waited for; matrix products, arithmetic and copies ran while one was open for 1% of the time, Pallas kernels for 11%

profile of v4, /device:TPU:10, one launch (start us, length us, event | category | flops | bytes accessed | tf_op | source)
XLA Modules:
  0.0 165.6 jit_solution(12310982916128186937)
XLA Ops:
  1.3 3.6 %pack.1 = (bf16[32,7296]{1,0:T(8,128)(2,1)S(1)}, bf16[32,7296]{1,0:T(8,128)(2,1)S(1)}, bf16[64,7296]{1,0:T(8,128)(2,1)}) custom-call(s32[2]{0:T(128)S(1)} %pad_add_fusion.place, s32[1,1024]{1,0:T(1,128)} %bitcast.23, s32[1,1024]{1,0:T(1,128)} %bitcast.24, f32[1,64]{1,0:T(1,128)} %bitcast.25, f32[1,64]{1,0:T(1,128)} %bitcast.26, bf16[64,7168]{1,0:T(8,128)(2,1)} %bitcast.21, ...), custom_call_target="tpu_custom_call" | custom-call | tf_op jit(solution)/shard_map/pack/pack/pallas_call | solution.py:128
  12.5 8.0 %collective-permute-done.a.refs_2_ = bf16[32,7296]{1,0:T(8,128)(2,1)S(1)} collective-permute-done((bf16[32,7296]{1,0:T(8,128)(2,1)S(1)}, bf16[32,7296]{1,0:T(8,128)(2,1)S(1)}, u32[]{:S(2)}, u32[]{:S(2)}) %collective-permute-start) | collective-permute-done | bytes 466976 | tf_op jit(solution)/shard_map/first1/ppermute | solution.py:33
  24.4 5.9 %collective-permute-done.4.refs_1_ = bf16[128,1792]{1,0:T(8,128)(2,1)S(1)} collective-permute-done((bf16[128,1792]{1,0:T(8,128)(2,1)S(1)}, bf16[128,1792]{1,0:T(8,128)(2,1)S(1)}, u32[]{:S(2)}, u32[]{:S(2)}) %collective-permute-start.4) | collective-permute-done | bytes 458784 | tf_op jit(solution)/shard_map/down/ppermute | solution.py:33
  34.3 5.6 %collective-permute-start.7 = (bf16[64,7296]{1,0:T(8,128)(2,1)S(1)}, bf16[64,7296]{1,0:T(8,128)(2,1)S(1)}, u32[]{:S(2)}, u32[]{:S(2)}) collective-permute-start(bf16[64,7296]{1,0:T(8,128)(2,1)S(1)} %get-tuple-element.56), channel_id=1, source_target_pairs={{0,6},{1,7},{2,0},{3,1},{4,2},{5,3},{6,4},{7,5},{8,14},{9,15},{10,... | collective-permute-start | bytes 2801672 | tf_op jit(solution)/shard_map/second1/ppermute | solution.py:33
  39.8 2.5 %collective-permute-done.8.refs_3_ = bf16[128,1792]{1,0:T(8,128)(2,1)S(1)} collective-permute-done((bf16[128,1792]{1,0:T(8,128)(2,1)S(1)}, bf16[128,1792]{1,0:T(8,128)(2,1)S(1)}, u32[]{:S(2)}, u32[]{:S(2)}) %collective-permute-start.8) | collective-permute-done | bytes 458784 | tf_op jit(solution)/shard_map/down/ppermute | solution.py:33
  46.4 14.9 %collective-permute-done.6.refs_4_ = bf16[64,7296]{1,0:T(8,128)(2,1)S(1)} collective-permute-done((bf16[64,7296]{1,0:T(8,128)(2,1)S(1)}, bf16[64,7296]{1,0:T(8,128)(2,1)S(1)}, u32[]{:S(2)}, u32[]{:S(2)}) %collective-permute-start.6) | collective-permute-done | bytes 933920 | tf_op jit(solution)/shard_map/second1/ppermute | solution.py:33
  61.4 3.5 %collective-permute-done.7.refs_5_ = bf16[64,7296]{1,0:T(8,128)(2,1)S(1)} collective-permute-done((bf16[64,7296]{1,0:T(8,128)(2,1)S(1)}, bf16[64,7296]{1,0:T(8,128)(2,1)S(1)}, u32[]{:S(2)}, u32[]{:S(2)}) %collective-permute-start.7) | collective-permute-done | bytes 933920 | tf_op jit(solution)/shard_map/second1/ppermute | solution.py:33
  64.9 3.7 %hidden.2.refs_6_ = bf16[256,256]{1,0:T(8,128)(2,1)S(1)} custom-call(bf16[32,7296]{1,0:T(8,128)(2,1)S(1)} %get-tuple-element.60.d.refs_0_, bf16[32,7296]{1,0:T(8,128)(2,1)S(1)} %get-tuple-element.61.b.refs_1_, bf16[32,7296]{1,0:T(8,128)(2,1)S(1)} %collective-permute-done.a.refs_2_, bf16[32,7296]{1,0:T(8,128)(2,1)} %collective-permute-done.1.c.refs_3_, ...), custom_call_target="tpu_custom_call" | custom-call | flops 1879048192 | bytes 11010048 | tf_op jit(solution)/shard_map/hidden1/hidden/pallas_call | solution.py:173
  70.9 2.6 %collective-permute-start.12 = (bf16[256,256]{1,0:T(8,128)(2,1)S(1)}, bf16[256,256]{1,0:T(8,128)(2,1)S(1)}, u32[]{:S(2)}, u32[]{:S(2)}) collective-permute-start(bf16[256,256]{1,0:T(8,128)(2,1)S(1)} %hidden.2.refs_6_), channel_id=1, source_target_pairs={{0,4},{1,5},{2,6},{3,7},{4,0},{5,1},{6,2},{7,3},{8,12},{9,13},{10,... | collective-permute-start | bytes 393224 | tf_op jit(solution)/shard_map/hidden1/ppermute | solution.py:33
  75.4 2.9 %collective-permute-done.12.refs_9_ = bf16[256,256]{1,0:T(8,128)(2,1)S(1)} collective-permute-done((bf16[256,256]{1,0:T(8,128)(2,1)S(1)}, bf16[256,256]{1,0:T(8,128)(2,1)S(1)}, u32[]{:S(2)}, u32[]{:S(2)}) %collective-permute-start.12) | collective-permute-done | bytes 131104 | tf_op jit(solution)/shard_map/hidden1/ppermute | solution.py:33
  82.8 3.1 %collective-permute-start.13 = (bf16[64,1792]{1,0:T(8,128)(2,1)S(1)}, bf16[64,1792]{1,0:T(8,128)(2,1)S(1)}, u32[]{:S(2)}, u32[]{:S(2)}) collective-permute-start(bf16[64,1792]{1,0:T(8,128)(2,1)S(1)} %get-tuple-element.67), channel_id=1, source_target_pairs={{0,6},{1,7},{2,0},{3,1},{4,2},{5,3},{6,4},{7,5},{8,14},{9,15},{10,... | collective-permute-start | bytes 688136 | tf_op jit(solution)/shard_map/back1/ppermute | solution.py:33
  85.9 10.5 %collective-permute-done.19.refs_4_ = bf16[64,7296]{1,0:T(8,128)(2,1)S(1)} collective-permute-done((bf16[64,7296]{1,0:T(8,128)(2,1)S(1)}, bf16[64,7296]{1,0:T(8,128)(2,1)S(1)}, u32[]{:S(2)}, u32[]{:S(2)}) %collective-permute-start.19) | collective-permute-done | bytes 933920 | tf_op jit(solution)/shard_map/second0/ppermute | solution.py:33
  96.4 5.3 %collective-permute-done.20.refs_5_ = bf16[64,7296]{1,0:T(8,128)(2,1)S(1)} collective-permute-done((bf16[64,7296]{1,0:T(8,128)(2,1)S(1)}, bf16[64,7296]{1,0:T(8,128)(2,1)S(1)}, u32[]{:S(2)}, u32[]{:S(2)}) %collective-permute-start.20) | collective-permute-done | bytes 933920 | tf_op jit(solution)/shard_map/second0/ppermute | solution.py:33
  101.6 3.6 %hidden.3.refs_6_ = bf16[256,256]{1,0:T(8,128)(2,1)S(1)} custom-call(bf16[32,7296]{1,0:T(8,128)(2,1)S(1)} %get-tuple-element.91.d.refs_0_, bf16[32,7296]{1,0:T(8,128)(2,1)S(1)} %get-tuple-element.90.b.refs_1_, bf16[32,7296]{1,0:T(8,128)(2,1)S(1)} %collective-permute-done.17.a.refs_2_, bf16[32,7296]{1,0:T(8,128)(2,1)S(1)} %collective-permute-done.18.c.refs_3_, ...), custom_call_target="tpu_custom_call" | custom-call | flops 1879048192 | bytes 11010048 | tf_op jit(solution)/shard_map/hidden0/hidden/pallas_call | solution.py:173
  111.1 2.8 %collective-permute-start.15 = (bf16[64,1792]{1,0:T(8,128)(2,1)S(1)}, bf16[64,1792]{1,0:T(8,128)(2,1)S(1)}, u32[]{:S(2)}, u32[]{:S(2)}) collective-permute-start(bf16[64,1792]{1,0:T(8,128)(2,1)S(1)} %get-tuple-element.69), channel_id=1, source_target_pairs={{0,4},{1,5},{2,6},{3,7},{4,0},{5,1},{6,2},{7,3},{8,12},{9,13},{10,... | collective-permute-start | bytes 688136 | tf_op jit(solution)/shard_map/back1/ppermute | solution.py:33
  114.0 2.5 %collective-permute-done.23.refs_9_ = bf16[256,256]{1,0:T(8,128)(2,1)S(1)} collective-permute-done((bf16[256,256]{1,0:T(8,128)(2,1)S(1)}, bf16[256,256]{1,0:T(8,128)(2,1)S(1)}, u32[]{:S(2)}, u32[]{:S(2)}) %collective-permute-start.23) | collective-permute-done | bytes 131104 | tf_op jit(solution)/shard_map/hidden0/ppermute | solution.py:33
  119.7 6.4 %collective-permute-start.28 = (bf16[64,1792]{1,0:T(8,128)(2,1)S(1)}, bf16[64,1792]{1,0:T(8,128)(2,1)S(1)}, u32[]{:S(2)}, u32[]{:S(2)}) collective-permute-start(bf16[64,1792]{1,0:T(8,128)(2,1)S(1)} %get-tuple-element.85), channel_id=1, source_target_pairs={{0,4},{1,5},{2,6},{3,7},{4,0},{5,1},{6,2},{7,3},{8,12},{9,13},{10,... | collective-permute-start | bytes 688136 | tf_op jit(solution)/shard_map/back0/ppermute | solution.py:33
  126.2 5.1 %collective-permute-start.24 = (bf16[32,7296]{1,0:T(8,128)(2,1)S(1)}, bf16[32,7296]{1,0:T(8,128)(2,1)S(1)}, u32[]{:S(2)}, u32[]{:S(2)}) collective-permute-start(bf16[32,7296]{1,0:T(8,128)(2,1)S(1)} %get-tuple-element.80), channel_id=1, source_target_pairs={{0,16},{1,17},{2,18},{3,19},{4,20},{5,21},{6,22},{7,23},{8,24},{9,... | collective-permute-start | bytes 1400840 | tf_op jit(solution)/shard_map/relay1/ppermute | solution.py:33
  131.3 4.0 %collective-permute-start.25 = (bf16[32,7296]{1,0:T(8,128)(2,1)S(1)}, bf16[32,7296]{1,0:T(8,128)(2,1)S(1)}, u32[]{:S(2)}, u32[]{:S(2)}) collective-permute-start(bf16[32,7296]{1,0:T(8,128)(2,1)S(1)} %get-tuple-element.81), channel_id=1, source_target_pairs={{16,0},{17,1},{18,2},{19,3},{20,4},{21,5},{22,6},{23,7},{24,8},{25... | collective-permute-start | bytes 1400840 | tf_op jit(solution)/shard_map/relay1/ppermute | solution.py:33
  136.1 3.9 %collective-permute-start.29 = (bf16[32,7296]{1,0:T(8,128)(2,1)S(1)}, bf16[32,7296]{1,0:T(8,128)(2,1)S(1)}, u32[]{:S(2)}, u32[]{:S(2)}) collective-permute-start(bf16[32,7296]{1,0:T(8,128)(2,1)S(1)} %get-tuple-element.86), channel_id=1, source_target_pairs={{0,24},{1,25},{2,26},{3,27},{4,28},{5,29},{6,30},{7,31},{8,16},{9,... | collective-permute-start | bytes 1400840 | tf_op jit(solution)/shard_map/relay0/ppermute | solution.py:33
  140.0 4.0 %collective-permute-start.30 = (bf16[32,7296]{1,0:T(8,128)(2,1)S(1)}, bf16[32,7296]{1,0:T(8,128)(2,1)S(1)}, u32[]{:S(2)}, u32[]{:S(2)}) collective-permute-start(bf16[32,7296]{1,0:T(8,128)(2,1)S(1)} %get-tuple-element.87), channel_id=1, source_target_pairs={{16,8},{17,9},{18,10},{19,11},{20,12},{21,13},{22,14},{23,15},{24,... | collective-permute-start | bytes 1400840 | tf_op jit(solution)/shard_map/relay0/ppermute | solution.py:33
  144.0 5.1 %collective-permute-done.24.refs_0_ = bf16[32,7296]{1,0:T(8,128)(2,1)S(1)} collective-permute-done((bf16[32,7296]{1,0:T(8,128)(2,1)S(1)}, bf16[32,7296]{1,0:T(8,128)(2,1)S(1)}, u32[]{:S(2)}, u32[]{:S(2)}) %collective-permute-start.24) | collective-permute-done | bytes 466976 | tf_op jit(solution)/shard_map/relay1/ppermute | solution.py:33
  149.3 6.4 %collective-permute-done.29.refs_2_ = bf16[32,7296]{1,0:T(8,128)(2,1)S(1)} collective-permute-done((bf16[32,7296]{1,0:T(8,128)(2,1)S(1)}, bf16[32,7296]{1,0:T(8,128)(2,1)S(1)}, u32[]{:S(2)}, u32[]{:S(2)}) %collective-permute-start.29) | collective-permute-done | bytes 466976 | tf_op jit(solution)/shard_map/relay0/ppermute | solution.py:33
  155.7 8.0 %collective-permute-done.30.refs_3_ = bf16[32,7296]{1,0:T(8,128)(2,1)S(1)} collective-permute-done((bf16[32,7296]{1,0:T(8,128)(2,1)S(1)}, bf16[32,7296]{1,0:T(8,128)(2,1)S(1)}, u32[]{:S(2)}, u32[]{:S(2)}) %collective-permute-start.30) | collective-permute-done | bytes 466976 | tf_op jit(solution)/shard_map/relay0/ppermute | solution.py:33
  (56 shorter events, 40.9 us)
Async XLA Ops:
  0.6 9.7 %collective-permute-start.2 = (bf16[7168,128]{1,0:T(8,128)(2,1)}, bf16[7168,128]{1,0:T(8,128)(2,1)S(1)}, u32[]{:S(2)}, u32[]{:S(2)}) collective-permute-start(bf16[7168,128]{1,0:T(8,128)(2,1)} %bitcast.14), channel_id=1, source_target_pairs={{0,1},{1,0},{2,3},{3,2},{4,5},{5,4},{6,7},{7,6},{8,9},{9,8},{10,11... | collective-permute-start | bytes 5505032 | tf_op jit(solution)/shard_map/weights/ppermute | solution.py:33
  4.9 38.1 %collective-permute-start.16 = (bf16[64,7296]{1,0:T(8,128)(2,1)}, bf16[64,7296]{1,0:T(8,128)(2,1)}, u32[]{:S(2)}, u32[]{:S(2)}) collective-permute-start(bf16[64,7296]{1,0:T(8,128)(2,1)} %get-tuple-element.70), channel_id=1, source_target_pairs={{0,8},{1,9},{2,10},{3,11},{4,12},{5,13},{6,14},{7,15},{8,0},{9,1},... | collective-permute-start | bytes 2801672 | tf_op jit(solution)/shard_map/swap/ppermute | solution.py:33
  6.9 13.6 %collective-permute-start = (bf16[32,7296]{1,0:T(8,128)(2,1)S(1)}, bf16[32,7296]{1,0:T(8,128)(2,1)S(1)}, u32[]{:S(2)}, u32[]{:S(2)}) collective-permute-start(bf16[32,7296]{1,0:T(8,128)(2,1)S(1)} %get-tuple-element.60.d.refs_0_), channel_id=1, source_target_pairs={{0,2},{1,3},{2,4},{3,5},{4,6},{5,7},{6,0},{7,1},{8,10},{9,11},{10,... | collective-permute-start | bytes 1400840 | tf_op jit(solution)/shard_map/first1/ppermute | solution.py:33
  8.4 13.7 %collective-permute-start.1 = (bf16[32,7296]{1,0:T(8,128)(2,1)S(1)}, bf16[32,7296]{1,0:T(8,128)(2,1)}, u32[]{:S(2)}, u32[]{:S(2)}) collective-permute-start(bf16[32,7296]{1,0:T(8,128)(2,1)S(1)} %get-tuple-element.61.b.refs_1_), channel_id=1, source_target_pairs={{0,6},{1,7},{2,0},{3,1},{4,2},{5,3},{6,4},{7,5},{8,14},{9,15},{10,... | collective-permute-start | bytes 1400840 | tf_op jit(solution)/shard_map/first1/ppermute | solution.py:33
  10.4 19.9 %collective-permute-start.4 = (bf16[128,1792]{1,0:T(8,128)(2,1)S(1)}, bf16[128,1792]{1,0:T(8,128)(2,1)S(1)}, u32[]{:S(2)}, u32[]{:S(2)}) collective-permute-start(bf16[128,1792]{1,0:T(8,128)(2,1)S(1)} %get-tuple-element.51), channel_id=1, source_target_pairs={{0,2},{1,3},{2,4},{3,5},{4,6},{5,7},{6,0},{7,1},{8,10},{9,11},{10,... | collective-permute-start | bytes 1376264 | tf_op jit(solution)/shard_map/down/ppermute | solution.py:33
  12.0 19.2 %collective-permute-start.5 = (bf16[128,1792]{1,0:T(8,128)(2,1)S(1)}, bf16[128,1792]{1,0:T(8,128)(2,1)S(1)}, u32[]{:S(2)}, u32[]{:S(2)}) collective-permute-start(bf16[128,1792]{1,0:T(8,128)(2,1)S(1)} %get-tuple-element.52), channel_id=1, source_target_pairs={{0,6},{1,7},{2,0},{3,1},{4,2},{5,3},{6,4},{7,5},{8,14},{9,15},{10,... | collective-permute-start | bytes 1376264 | tf_op jit(solution)/shard_map/down/ppermute | solution.py:33
  22.1 20.2 %collective-permute-start.8 = (bf16[128,1792]{1,0:T(8,128)(2,1)S(1)}, bf16[128,1792]{1,0:T(8,128)(2,1)S(1)}, u32[]{:S(2)}, u32[]{:S(2)}) collective-permute-start(bf16[128,1792]{1,0:T(8,128)(2,1)S(1)} %get-tuple-element.59), channel_id=1, source_target_pairs={{0,4},{1,5},{2,6},{3,7},{4,0},{5,1},{6,2},{7,3},{8,12},{9,13},{10,... | collective-permute-start | bytes 1376264 | tf_op jit(solution)/shard_map/down/ppermute | solution.py:33
  32.3 29.0 %collective-permute-start.6 = (bf16[64,7296]{1,0:T(8,128)(2,1)S(1)}, bf16[64,7296]{1,0:T(8,128)(2,1)S(1)}, u32[]{:S(2)}, u32[]{:S(2)}) collective-permute-start(bf16[64,7296]{1,0:T(8,128)(2,1)S(1)} %get-tuple-element.55), channel_id=1, source_target_pairs={{0,2},{1,3},{2,4},{3,5},{4,6},{5,7},{6,0},{7,1},{8,10},{9,11},{10,... | collective-permute-start | bytes 2801672 | tf_op jit(solution)/shard_map/second1/ppermute | solution.py:33
  34.3 30.6 %collective-permute-start.7 = (bf16[64,7296]{1,0:T(8,128)(2,1)S(1)}, bf16[64,7296]{1,0:T(8,128)(2,1)S(1)}, u32[]{:S(2)}, u32[]{:S(2)}) collective-permute-start(bf16[64,7296]{1,0:T(8,128)(2,1)S(1)} %get-tuple-element.56), channel_id=1, source_target_pairs={{0,6},{1,7},{2,0},{3,1},{4,2},{5,3},{6,4},{7,5},{8,14},{9,15},{10,... | collective-permute-start | bytes 2801672 | tf_op jit(solution)/shard_map/second1/ppermute | solution.py:33
  42.9 22.0 %collective-permute-start.9 = (bf16[512,1792]{1,0:T(8,128)(2,1)S(1)}, bf16[512,1792]{1,0:T(8,128)(2,1)S(1)}, u32[]{:S(2)}, u32[]{:S(2)}) collective-permute-start(bf16[512,1792]{1,0:T(8,128)(2,1)S(1)} %stack.13.refs_10_), channel_id=1, source_target_pairs={{0,1},{1,0},{2,3},{3,2},{4,5},{5,4},{6,7},{7,6},{8,9},{9,8},{10,11... | collective-permute-start | bytes 5505032 | tf_op jit(solution)/shard_map/down/ppermute | solution.py:33
  44.3 29.2 %collective-permute-start.17 = (bf16[32,7296]{1,0:T(8,128)(2,1)S(1)}, bf16[32,7296]{1,0:T(8,128)(2,1)S(1)}, u32[]{:S(2)}, u32[]{:S(2)}) collective-permute-start(bf16[32,7296]{1,0:T(8,128)(2,1)S(1)} %get-tuple-element.91.d.refs_0_), channel_id=1, source_target_pairs={{0,2},{1,3},{2,4},{3,5},{4,6},{5,7},{6,0},{7,1},{8,10},{9,11},{10,... | collective-permute-start | bytes 1400840 | tf_op jit(solution)/shard_map/first0/ppermute | solution.py:33
  45.4 28.3 %collective-permute-start.18 = (bf16[32,7296]{1,0:T(8,128)(2,1)S(1)}, bf16[32,7296]{1,0:T(8,128)(2,1)S(1)}, u32[]{:S(2)}, u32[]{:S(2)}) collective-permute-start(bf16[32,7296]{1,0:T(8,128)(2,1)S(1)} %get-tuple-element.90.b.refs_1_), channel_id=1, source_target_pairs={{0,6},{1,7},{2,0},{3,1},{4,2},{5,3},{6,4},{7,5},{8,14},{9,15},{10,... | collective-permute-start | bytes 1400840 | tf_op jit(solution)/shard_map/first0/ppermute | solution.py:33
  78.4 17.9 %collective-permute-start.19 = (bf16[64,7296]{1,0:T(8,128)(2,1)S(1)}, bf16[64,7296]{1,0:T(8,128)(2,1)S(1)}, u32[]{:S(2)}, u32[]{:S(2)}) collective-permute-start(bf16[64,7296]{1,0:T(8,128)(2,1)S(1)} %get-tuple-element.74), channel_id=1, source_target_pairs={{0,2},{1,3},{2,4},{3,5},{4,6},{5,7},{6,0},{7,1},{8,10},{9,11},{10,... | collective-permute-start | bytes 2801672 | tf_op jit(solution)/shard_map/second0/ppermute | solution.py:33
  80.6 21.1 %collective-permute-start.20 = (bf16[64,7296]{1,0:T(8,128)(2,1)S(1)}, bf16[64,7296]{1,0:T(8,128)(2,1)S(1)}, u32[]{:S(2)}, u32[]{:S(2)}) collective-permute-start(bf16[64,7296]{1,0:T(8,128)(2,1)S(1)} %get-tuple-element.75), channel_id=1, source_target_pairs={{0,6},{1,7},{2,0},{3,1},{4,2},{5,3},{6,4},{7,5},{8,14},{9,15},{10,... | collective-permute-start | bytes 2801672 | tf_op jit(solution)/shard_map/second0/ppermute | solution.py:33
  82.8 37.0 %collective-permute-start.13 = (bf16[64,1792]{1,0:T(8,128)(2,1)S(1)}, bf16[64,1792]{1,0:T(8,128)(2,1)S(1)}, u32[]{:S(2)}, u32[]{:S(2)}) collective-permute-start(bf16[64,1792]{1,0:T(8,128)(2,1)S(1)} %get-tuple-element.67), channel_id=1, source_target_pairs={{0,6},{1,7},{2,0},{3,1},{4,2},{5,3},{6,4},{7,5},{8,14},{9,15},{10,... | collective-permute-start | bytes 688136 | tf_op jit(solution)/shard_map/back1/ppermute | solution.py:33
  109.6 16.5 %collective-permute-start.14 = (bf16[64,1792]{1,0:T(8,128)(2,1)S(1)}, bf16[64,1792]{1,0:T(8,128)(2,1)S(1)}, u32[]{:S(2)}, u32[]{:S(2)}) collective-permute-start(bf16[64,1792]{1,0:T(8,128)(2,1)S(1)} %get-tuple-element.68), channel_id=1, source_target_pairs={{0,2},{1,3},{2,4},{3,5},{4,6},{5,7},{6,0},{7,1},{8,10},{9,11},{10,... | collective-permute-start | bytes 688136 | tf_op jit(solution)/shard_map/back1/ppermute | solution.py:33
  111.1 15.0 %collective-permute-start.15 = (bf16[64,1792]{1,0:T(8,128)(2,1)S(1)}, bf16[64,1792]{1,0:T(8,128)(2,1)S(1)}, u32[]{:S(2)}, u32[]{:S(2)}) collective-permute-start(bf16[64,1792]{1,0:T(8,128)(2,1)S(1)} %get-tuple-element.69), channel_id=1, source_target_pairs={{0,4},{1,5},{2,6},{3,7},{4,0},{5,1},{6,2},{7,3},{8,12},{9,13},{10,... | collective-permute-start | bytes 688136 | tf_op jit(solution)/shard_map/back1/ppermute | solution.py:33
  117.6 17.6 %collective-permute-start.26 = (bf16[64,1792]{1,0:T(8,128)(2,1)S(1)}, bf16[64,1792]{1,0:T(8,128)(2,1)S(1)}, u32[]{:S(2)}, u32[]{:S(2)}) collective-permute-start(bf16[64,1792]{1,0:T(8,128)(2,1)S(1)} %get-tuple-element.83), channel_id=1, source_target_pairs={{0,6},{1,7},{2,0},{3,1},{4,2},{5,3},{6,4},{7,5},{8,14},{9,15},{10,... | collective-permute-start | bytes 688136 | tf_op jit(solution)/shard_map/back0/ppermute | solution.py:33
  118.7 16.5 %collective-permute-start.27 = (bf16[64,1792]{1,0:T(8,128)(2,1)S(1)}, bf16[64,1792]{1,0:T(8,128)(2,1)S(1)}, u32[]{:S(2)}, u32[]{:S(2)}) collective-permute-start(bf16[64,1792]{1,0:T(8,128)(2,1)S(1)} %get-tuple-element.84), channel_id=1, source_target_pairs={{0,2},{1,3},{2,4},{3,5},{4,6},{5,7},{6,0},{7,1},{8,10},{9,11},{10,... | collective-permute-start | bytes 688136 | tf_op jit(solution)/shard_map/back0/ppermute | solution.py:33
  119.7 15.5 %collective-permute-start.28 = (bf16[64,1792]{1,0:T(8,128)(2,1)S(1)}, bf16[64,1792]{1,0:T(8,128)(2,1)S(1)}, u32[]{:S(2)}, u32[]{:S(2)}) collective-permute-start(bf16[64,1792]{1,0:T(8,128)(2,1)S(1)} %get-tuple-element.85), channel_id=1, source_target_pairs={{0,4},{1,5},{2,6},{3,7},{4,0},{5,1},{6,2},{7,3},{8,12},{9,13},{10,... | collective-permute-start | bytes 688136 | tf_op jit(solution)/shard_map/back0/ppermute | solution.py:33
  126.2 23.0 %collective-permute-start.24 = (bf16[32,7296]{1,0:T(8,128)(2,1)S(1)}, bf16[32,7296]{1,0:T(8,128)(2,1)S(1)}, u32[]{:S(2)}, u32[]{:S(2)}) collective-permute-start(bf16[32,7296]{1,0:T(8,128)(2,1)S(1)} %get-tuple-element.80), channel_id=1, source_target_pairs={{0,16},{1,17},{2,18},{3,19},{4,20},{5,21},{6,22},{7,23},{8,24},{9,... | collective-permute-start | bytes 1400840 | tf_op jit(solution)/shard_map/relay1/ppermute | solution.py:33
  131.3 18.1 %collective-permute-start.25 = (bf16[32,7296]{1,0:T(8,128)(2,1)S(1)}, bf16[32,7296]{1,0:T(8,128)(2,1)S(1)}, u32[]{:S(2)}, u32[]{:S(2)}) collective-permute-start(bf16[32,7296]{1,0:T(8,128)(2,1)S(1)} %get-tuple-element.81), channel_id=1, source_target_pairs={{16,0},{17,1},{18,2},{19,3},{20,4},{21,5},{22,6},{23,7},{24,8},{25... | collective-permute-start | bytes 1400840 | tf_op jit(solution)/shard_map/relay1/ppermute | solution.py:33
  136.1 19.7 %collective-permute-start.29 = (bf16[32,7296]{1,0:T(8,128)(2,1)S(1)}, bf16[32,7296]{1,0:T(8,128)(2,1)S(1)}, u32[]{:S(2)}, u32[]{:S(2)}) collective-permute-start(bf16[32,7296]{1,0:T(8,128)(2,1)S(1)} %get-tuple-element.86), channel_id=1, source_target_pairs={{0,24},{1,25},{2,26},{3,27},{4,28},{5,29},{6,30},{7,31},{8,16},{9,... | collective-permute-start | bytes 1400840 | tf_op jit(solution)/shard_map/relay0/ppermute | solution.py:33
  140.0 23.8 %collective-permute-start.30 = (bf16[32,7296]{1,0:T(8,128)(2,1)S(1)}, bf16[32,7296]{1,0:T(8,128)(2,1)S(1)}, u32[]{:S(2)}, u32[]{:S(2)}) collective-permute-start(bf16[32,7296]{1,0:T(8,128)(2,1)S(1)} %get-tuple-element.87), channel_id=1, source_target_pairs={{16,8},{17,9},{18,10},{19,11},{20,12},{21,13},{22,14},{23,15},{24,... | collective-permute-start | bytes 1400840 | tf_op jit(solution)/shard_map/relay0/ppermute | solution.py:33
  (9 other events, 95.1 us)
